TPU v7x, 32 devices: a whole 2x2x4 slice. The times are simulated.
32 devices in a mesh: batch: 4 (over y, x), blk: 8 (over z, core).
Axes of the slice: x: 2, y: 2, z: 4, core: 2. Of those that a mesh axis runs over, the one named last changes fastest.
Arguments:
- tokens: bfloat16 [4, 4096, 768], P('batch', 'blk'), may hold values from -6 to 6
- lengths: int32 [4, 3], P('batch'), may hold values from 128 to 3839, as said below
- norm_one: bfloat16 [768], P(('batch', 'blk')), may hold values from 0.5 to 1.5
- w_qkv: bfloat16 [768, 2304], P(('batch', 'blk')), may hold values from -0.109375 to 0.109375
- rel_table: float32 [32, 12], replicated, may hold values from -4 to 4
- w_out: bfloat16 [768, 768], P(('batch', 'blk')), may hold values from -6 to 6
- norm_two: bfloat16 [768], P(('batch', 'blk')), may hold values from 0.5 to 1.5
- w_gateup: bfloat16 [768, 4096], P(('batch', 'blk')), may hold values from -0.21875 to 0.21875
- w_down: bfloat16 [2048, 768], P(('batch', 'blk')), may hold values from -0.125 to 0.125
- cotangent: bfloat16 [4, 4096, 768], P('batch', 'blk'), may hold values from -6 to 6
- row_qkv: float32 [768], P(('batch', 'blk')), may hold values from 0.25 to 4
- col_qkv: float32 [2304], replicated, may hold values from 0.25 to 4
- row_out: float32 [768], P(('batch', 'blk')), may hold values from 0.25 to 4
- col_out: float32 [768], replicated, may hold values from 0.25 to 4
- row_gateup: float32 [768], P(('batch', 'blk')), may hold values from 0.25 to 4
- col_gateup: float32 [4096], replicated, may hold values from 0.25 to 4
- row_down: float32 [2048], P(('batch', 'blk')), may hold values from 0.25 to 4
- col_down: float32 [768], replicated, may hold values from 0.25 to 4
Outputs:
- output: bfloat16 [4, 4096, 768], P('batch', 'blk')
- d_tokens: bfloat16 [4, 4096, 768], P('batch', 'blk')
- d_norm_one: float32 [768], P(('batch', 'blk'))
- d_qkv: float32 [768, 2304], P(('batch', 'blk'))
- d_table: float32 [32, 12], replicated
- d_out: float32 [768, 768], P(('batch', 'blk'))
- d_norm_two: float32 [768], P(('batch', 'blk'))
- d_gateup: float32 [768, 4096], P(('batch', 'blk'))
- d_down: float32 [2048, 768], P(('batch', 'blk'))
- new_row_qkv: float32 [768], P(('batch', 'blk'))
- new_col_qkv: float32 [2304], replicated
- new_row_out: float32 [768], P(('batch', 'blk'))
- new_col_out: float32 [768], replicated
- new_row_gateup: float32 [768], P(('batch', 'blk'))
- new_col_gateup: float32 [4096], replicated
- new_row_down: float32 [2048], P(('batch', 'blk'))
- new_col_down: float32 [768], replicated
Inputs may be any that keep to these rules, and one draw needn't show every extreme that they name: `lengths`: each row holds 3 documents one after the other from position 0, then 1 to 128 padding positions at the end. The first document is shorter than 512; the third is 128 to 256 long, so the second document begins on the first device of blk and ends on the last.
All inputs are finite; a program needn't handle non-finite values.
Results may differ from a plain program's by a relative error of at most 0.022.
Values may be sent and summed in bfloat16 or wider, within the bound.
No kernel may reach another device: no remote copies, remote signals or barrier semaphores. Data moves between devices by JAX's collectives and lax.ppermute only.
A program may use at most 192 MiB of HBM per device.

v0:
```python
import math

import jax
import jax.numpy as jnp
from jax import lax
from jax.sharding import PartitionSpec as P

BUCKETS = 32


THRESHOLDS = (12, 16, 23, 32, 46, 64, 91)
EPSILON = 1e-06
DECAY_RATE = 0.5
NEGATIVE = -1000000000.0
GELU_SCALE = 0.7978845608028654


def from_behind(shard, axis, by):
    peers = lax.axis_size(axis)
    return lax.ppermute(shard, axis, [(i, (i + by) % peers) for i in range(peers)])


def bucket_of(offset):
    distance = jnp.abs(offset)
    steps_up = 8 + sum(((distance >= limit).astype(jnp.int32) for limit in THRESHOLDS))
    within = jnp.where(distance < 8, distance, steps_up)
    return within + 16 * (offset > 0).astype(jnp.int32)


def documents(length_row, positions):
    ends = jnp.cumsum(length_row)
    segment = jnp.sum((positions[:, None] >= ends[None, :]).astype(jnp.int32), axis=1)
    return (segment, positions >= ends[-1])


def pair_layout(query_pos, key_pos, length_row):
    query_seg, query_pad = documents(length_row, query_pos)
    key_seg, key_pad = documents(length_row, key_pos)
    allowed = (query_seg[:, None] == key_seg[None, :]) & ~key_pad[None, :] | (
        query_pos[:, None] == key_pos[None, :]
    )
    return (allowed, bucket_of(key_pos[None, :] - query_pos[:, None]))


def bias_of(bucket, table):
    total = jnp.zeros((table.shape[1],) + bucket.shape, jnp.float32)
    for label in range(table.shape[0]):
        total = jnp.where(bucket[None] == label, table[label][:, None, None], total)
    return total


def rms_scale(values, gain):
    return values * lax.rsqrt(jnp.mean(values * values, axis=-1, keepdims=True) + EPSILON) * gain


def gelu_tanh(values):
    return (
        0.5 * values * (1.0 + jnp.tanh(GELU_SCALE * (values + 0.044715 * values * values * values)))
    )


def gated(gate, upward):
    return gelu_tanh(gate) * upward


def inner_first(left, right):
    return lax.dot_general(
        left, right, (((0,), (0,)), ((), ())), preferred_element_type=jnp.float32
    )


def inner_last(left, right):
    return lax.dot_general(
        left, right, (((1,), (1,)), ((), ())), preferred_element_type=jnp.float32
    )


def pair_grads(
    query_rows,
    dctx_rows,
    log_total,
    delta,
    query_pos,
    key_rows,
    value_rows,
    key_pos,
    length_row,
    table,
):
    allowed, bucket = pair_layout(query_pos, key_pos, length_row)
    heads = table.shape[1]
    row_count = query_rows.shape[0]
    key_count = key_rows.shape[0]
    width = query_rows.shape[1]
    head_size = width // heads
    query3 = query_rows.reshape(row_count, heads, head_size)
    dctx3 = dctx_rows.reshape(row_count, heads, head_size)
    key3 = key_rows.reshape(key_count, heads, head_size)
    value3 = value_rows.reshape(key_count, heads, head_size)
    scores = jnp.einsum("qhd,khd->hqk", query3, key3, preferred_element_type=jnp.float32) + bias_of(
        bucket, table
    )
    weights = jnp.where(allowed[None], jnp.exp(scores - log_total[:, :, None]), 0.0)
    dprob = jnp.einsum("qhd,khd->hqk", dctx3, value3, preferred_element_type=jnp.float32)
    dscores = (weights * (dprob - delta[:, :, None])).astype(jnp.bfloat16)
    grad_query = jnp.einsum(
        "hqk,khd->qhd", dscores, key3, preferred_element_type=jnp.float32
    ).reshape(row_count, width)
    grad_key = jnp.einsum(
        "hqk,qhd->khd", dscores, query3, preferred_element_type=jnp.float32
    ).reshape(key_count, width)
    grad_value = jnp.einsum(
        "hqk,qhd->khd", weights.astype(jnp.bfloat16), dctx3, preferred_element_type=jnp.float32
    ).reshape(key_count, width)
    labels = jnp.arange(table.shape[0], dtype=jnp.int32)
    onehot = (bucket[:, :, None] == labels[None, None, :]).astype(jnp.bfloat16)
    table_grad = jnp.einsum("hqk,qkb->bh", dscores, onehot, preferred_element_type=jnp.float32)
    return (grad_query, grad_key, grad_value, table_grad)


def factored(grad_shard, column_total, row_old, column_old, row_total):
    columns = grad_shard.shape[1]
    mean_square = jnp.sum(column_total) / (row_total * columns) + EPSILON
    row_new = (
        DECAY_RATE * row_old
        + (1.0 - DECAY_RATE) * (jnp.sum(grad_shard * grad_shard, axis=1) / columns) / mean_square
    )
    column_new = (
        DECAY_RATE * column_old + (1.0 - DECAY_RATE) * (column_total / row_total) / mean_square
    )
    return (row_new, column_new)


def shards(
    tokens,
    lengths,
    norm_one,
    w_qkv,
    rel_table,
    w_out,
    norm_two,
    w_gateup,
    w_down,
    cotangent,
    row_qkv,
    col_qkv,
    row_out,
    col_out,
    row_gateup,
    col_gateup,
    row_down,
    col_down,
):
    inputs = tokens[0].astype(jnp.float32)
    tok_rows = inputs.shape[0]
    cycle_size = lax.axis_size("blk")
    cycle_place = lax.axis_index("blk")
    length_row = lengths[0]
    row_range = jnp.arange(tok_rows, dtype=jnp.int32)
    positions = cycle_place * tok_rows + row_range
    gain_one, full_qkv, full_out, gain_two, full_gateup, full_down = (
        lax.all_gather(norm_one, ("batch", "blk"), axis=0, tiled=True),
        lax.all_gather(w_qkv, ("batch", "blk"), axis=0, tiled=True),
        lax.all_gather(w_out, ("batch", "blk"), axis=0, tiled=True),
        lax.all_gather(norm_two, ("batch", "blk"), axis=0, tiled=True),
        lax.all_gather(w_gateup, ("batch", "blk"), axis=0, tiled=True),
        lax.all_gather(w_down, ("batch", "blk"), axis=0, tiled=True),
    )
    gain_one = gain_one.astype(jnp.float32)
    gain_two = gain_two.astype(jnp.float32)
    heads = rel_table.shape[1]
    width = full_out.shape[0]
    head_size = width // heads
    normed = rms_scale(inputs, gain_one).astype(jnp.bfloat16)
    qkv = jnp.dot(normed, full_qkv, preferred_element_type=jnp.float32).astype(jnp.bfloat16)
    query = qkv[:, :width]
    keys = qkv[:, width : 2 * width]
    values = qkv[:, 2 * width :]
    query3 = query.reshape(tok_rows, heads, head_size)
    start_state = (
        jnp.full((heads, tok_rows), NEGATIVE, jnp.float32),
        jnp.zeros((heads, tok_rows), jnp.float32),
        jnp.zeros((heads, tok_rows, head_size), jnp.float32),
    )
    piece_keys = lax.all_gather(keys, "blk", axis=0, tiled=True)
    piece_values = lax.all_gather(values, "blk", axis=0, tiled=True)
    count = piece_keys.shape[0]
    block = math.gcd(count, tok_rows)

    def one_block(block_index, state):
        best, totals, accum = state
        key_block = lax.dynamic_slice_in_dim(piece_keys, block_index * block, block, 0).reshape(
            block, heads, head_size
        )
        value_block = lax.dynamic_slice_in_dim(piece_values, block_index * block, block, 0).reshape(
            block, heads, head_size
        )
        key_pos = block_index * block + jnp.arange(block, dtype=jnp.int32)
        allowed, bucket = pair_layout(positions, key_pos, length_row)
        scores = jnp.einsum(
            "qhd,khd->hqk", query3, key_block, preferred_element_type=jnp.float32
        ) + bias_of(bucket, rel_table)
        scores = jnp.where(allowed[None], scores, NEGATIVE)
        new_max = jnp.maximum(best, jnp.max(scores, axis=2))
        factor = jnp.exp(best - new_max)
        unnorm = jnp.where(allowed[None], jnp.exp(scores - new_max[:, :, None]), 0.0)
        totals = totals * factor + jnp.sum(unnorm, axis=2)
        added = jnp.einsum(
            "hqk,khd->hqd",
            unnorm.astype(jnp.bfloat16),
            value_block,
            preferred_element_type=jnp.float32,
        )
        accum = accum * factor[:, :, None] + added
        return (new_max, totals, accum)

    best, totals, accum = lax.fori_loop(0, count // block, one_block, start_state)
    context = accum / totals[:, :, None]
    log_total = best + jnp.log(totals)
    context_rows = jnp.transpose(context, (1, 0, 2)).reshape(tok_rows, width).astype(jnp.bfloat16)
    mixed = inputs + jnp.dot(context_rows, full_out, preferred_element_type=jnp.float32)
    normed_two = rms_scale(mixed, gain_two).astype(jnp.bfloat16)
    gate_up = jnp.dot(normed_two, full_gateup, preferred_element_type=jnp.float32)
    hidden_units = gate_up.shape[1] // 2
    gate = gate_up[:, :hidden_units]
    upward = gate_up[:, hidden_units:]
    hidden = gated(gate, upward).astype(jnp.bfloat16)
    result = (mixed + jnp.dot(hidden, full_down, preferred_element_type=jnp.float32)).astype(
        jnp.bfloat16
    )
    upstream = cotangent[0]
    d_hidden = inner_last(upstream, full_down)
    grad_down = inner_first(hidden, upstream)
    gated_back = jax.vjp(gated, gate, upward)[1]
    d_gate, d_upward = gated_back(d_hidden)
    grad_act = jnp.concatenate([d_gate, d_upward], axis=1).astype(jnp.bfloat16)
    grad_gateup = inner_first(normed_two, grad_act)
    d_normed_two = inner_last(grad_act, full_gateup)
    norm_back_two = jax.vjp(rms_scale, mixed, gain_two)[1]
    d_mixed_norm, grad_gain_two = norm_back_two(d_normed_two)
    d_mixed = upstream.astype(jnp.float32) + d_mixed_norm
    d_branch = d_mixed.astype(jnp.bfloat16)
    grad_out = inner_first(context_rows, d_branch)
    d_context = inner_last(d_branch, full_out).astype(jnp.bfloat16)
    delta = jnp.einsum(
        "qhd,hqd->hq", d_context.astype(jnp.float32).reshape(tok_rows, heads, head_size), context
    )

    def key_turn(step_index, state):
        moving_keys, moving_values, key_grad, value_grad, query_grad, table_grad = state
        source = (cycle_place - step_index) % cycle_size
        grads = pair_grads(
            query,
            d_context,
            log_total,
            delta,
            positions,
            moving_keys,
            moving_values,
            source * tok_rows + row_range,
            length_row,
            rel_table,
        )
        return (
            moving_keys,
            moving_values,
            key_grad + grads[1],
            value_grad + grads[2],
            query_grad + grads[0],
            table_grad + grads[3],
        )

    def key_step(step_index, state):
        moving_keys, moving_values, key_grad, value_grad, query_grad, table_grad = key_turn(
            step_index, state
        )
        moving_keys, moving_values = from_behind((moving_keys, moving_values), "blk", 1)
        key_grad, value_grad = (
            from_behind(key_grad.astype(jnp.bfloat16), "blk", 1).astype(key_grad.dtype),
            from_behind(value_grad.astype(jnp.bfloat16), "blk", 1).astype(value_grad.dtype),
        )
        return (moving_keys, moving_values, key_grad, value_grad, query_grad, table_grad)

    zero_rows = jnp.zeros((tok_rows, width), jnp.float32)
    state = (
        keys,
        values,
        zero_rows,
        zero_rows,
        zero_rows,
        jnp.zeros((BUCKETS, heads), jnp.float32),
    )
    state = lax.fori_loop(0, cycle_size - 1, key_step, state)
    moving_keys, moving_values, key_grad, value_grad, query_grad, table_grad = key_turn(
        cycle_size - 1, state
    )
    key_grad, value_grad = (
        from_behind(key_grad.astype(jnp.bfloat16), "blk", 1).astype(key_grad.dtype),
        from_behind(value_grad.astype(jnp.bfloat16), "blk", 1).astype(value_grad.dtype),
    )
    d_qkv_rows = jnp.concatenate([query_grad, key_grad, value_grad], axis=1).astype(jnp.bfloat16)
    grad_qkv = inner_first(normed, d_qkv_rows)
    d_normed = inner_last(d_qkv_rows, full_qkv)
    norm_back_one = jax.vjp(rms_scale, inputs, gain_one)[1]
    d_inputs_norm, grad_gain_one = norm_back_one(d_normed)
    d_inputs = (d_mixed + d_inputs_norm).astype(jnp.bfloat16)
    shard_gain_one, shard_qkv, shard_out, shard_gain_two, shard_gateup, shard_down = (
        lax.psum_scatter(grad_gain_one, ("batch", "blk"), scatter_dimension=0, tiled=True),
        lax.psum_scatter(grad_qkv, ("batch", "blk"), scatter_dimension=0, tiled=True),
        lax.psum_scatter(grad_out, ("batch", "blk"), scatter_dimension=0, tiled=True),
        lax.psum_scatter(grad_gain_two, ("batch", "blk"), scatter_dimension=0, tiled=True),
        lax.psum_scatter(grad_gateup, ("batch", "blk"), scatter_dimension=0, tiled=True),
        lax.psum_scatter(grad_down, ("batch", "blk"), scatter_dimension=0, tiled=True),
    )
    table_total, column_qkv, column_out, column_gateup, column_down = lax.psum(
        (
            table_grad,
            jnp.sum(shard_qkv * shard_qkv, axis=0),
            jnp.sum(shard_out * shard_out, axis=0),
            jnp.sum(shard_gateup * shard_gateup, axis=0),
            jnp.sum(shard_down * shard_down, axis=0),
        ),
        ("batch", "blk"),
    )
    new_row_qkv, new_col_qkv = factored(shard_qkv, column_qkv, row_qkv, col_qkv, full_qkv.shape[0])
    new_row_out, new_col_out = factored(shard_out, column_out, row_out, col_out, full_out.shape[0])
    new_row_gateup, new_col_gateup = factored(
        shard_gateup, column_gateup, row_gateup, col_gateup, full_gateup.shape[0]
    )
    new_row_down, new_col_down = factored(
        shard_down, column_down, row_down, col_down, full_down.shape[0]
    )
    return (
        result[None],
        d_inputs[None],
        shard_gain_one,
        shard_qkv,
        table_total,
        shard_out,
        shard_gain_two,
        shard_gateup,
        shard_down,
        new_row_qkv,
        new_col_qkv,
        new_row_out,
        new_col_out,
        new_row_gateup,
        new_col_gateup,
        new_row_down,
        new_col_down,
    )


def solution(mesh):
    return jax.shard_map(
        shards,
        mesh=mesh,
        in_specs=(
            P("batch", "blk", None),
            P("batch", None),
            P(("batch", "blk")),
            P(("batch", "blk"), None),
            P(),
            P(("batch", "blk"), None),
            P(("batch", "blk")),
            P(("batch", "blk"), None),
            P(("batch", "blk"), None),
            P("batch", "blk", None),
            P(("batch", "blk")),
            P(),
            P(("batch", "blk")),
            P(),
            P(("batch", "blk")),
            P(),
            P(("batch", "blk")),
            P(),
        ),
        out_specs=(
            P("batch", "blk", None),
            P("batch", "blk", None),
            P(("batch", "blk")),
            P(("batch", "blk"), None),
            P(),
            P(("batch", "blk"), None),
            P(("batch", "blk")),
            P(("batch", "blk"), None),
            P(("batch", "blk"), None),
            P(("batch", "blk")),
            P(),
            P(("batch", "blk")),
            P(),
            P(("batch", "blk")),
            P(),
            P(("batch", "blk")),
            P(),
        ),
        check_vma=False,
    )
```

profile of v0, /device:TPU:0, one launch (start us, length us, event | category | flops | bytes accessed | tf_op | source)
XLA Modules:
  0.0 1921.7 jit_solution(11315112517353454618)
XLA Ops:
  9.7 42.3 %all-reduce.5 = (bf16[768]{0:T(1024)(128)(2,1)S(1)}, bf16[768]{0:T(1024)(128)(2,1)S(1)}) all-reduce(bf16[768]{0:T(1024)(128)(2,1)S(1)} %dynamic-update-slice, bf16[768]{0:T(1024)(128)(2,1)S(1)} %dynamic-update-slice.1), channel_id=1, replica_groups=mesh['batch'=4,'blk'=8] {'batch','blk'}, use_global_device_ids=true, to_apply=%add | all-reduce | flops 1536 | bytes 6144
  53.9 20.1 %all-gather.7.cloned.1.call-done = bf16[768,2304]{1,0:T(8,128)(2,1)} async-done(((bf16[24,2304]{1,0:T(8,128)(2,1)}), bf16[768,2304]{1,0:T(8,128)(2,1)}) %all-gather.7.cloned.1.call-update) | async-done | bytes 3538960 | tf_op jit(solution)/shard_map/all_gather | solution.py:163
  86.8 56.7 %all-gather.9.cloned.1.call-done = bf16[4096,768]{1,0:T(8,128)(2,1)} async-done(((bf16[512,768]{1,0:T(8,128)(2,1)}), bf16[4096,768]{1,0:T(8,128)(2,1)}) %all-gather.9.cloned.1.call-update) | async-done | bytes 6291472 | tf_op jit(solution)/shard_map/all_gather | solution.py:185
  143.4 65.7 %all-gather.11.cloned.1.call-done = bf16[4096,768]{1,0:T(8,128)(2,1)} async-done(((bf16[512,768]{1,0:T(8,128)(2,1)}), bf16[4096,768]{1,0:T(8,128)(2,1)}) %all-gather.11.cloned.1.call-update) | async-done | bytes 6291472 | tf_op jit(solution)/shard_map/all_gather | solution.py:186
  209.1 535.4 %while.46 = (s32[]{:T(128)}, f32[12,512]{1,0:T(8,128)S(1)}, f32[12,512]{1,0:T(8,128)S(1)}, f32[12,512,64]{1,2,0:T(8,128)}, s32[3,1]{0,1:T(1,128)S(1)}, /*index=5...) while((s32[]{:T(128)}, f32[12,512]{1,0:T(8,128)S(1)}, ...), condition=%wide.region_7.8_spmd.clone, body=%wide.region_2.7_spmd.clone.sunk | while | flops 952279552 | bytes 67790568 | solution.py:217
  227.0 8.1 compare_or_fusion.5
  237.5 37.0 %fusion.170 = (f32[12,512]{1,0:T(8,128)S(1)}, f32[12,512,512]{1,2,0:T(8,128)}) fusion(f32[12]{0:T(128)S(1)} %get-tuple-element.1403, pred[512,512]{0,1:T(8,128)(4,1)} %get-tuple-element.1408, f32[12]{0:T(128)S(1)} %get-tuple-element.1409, pred[512,512]{0,1:T(8,128)(4,1)} %get-tuple-element.1410, f32[12]{0:T(128)S(1)} %get-tuple-element.1411, ...), kind=kOutput, calls=%fused_computation.376.clone.1 | convolution fusion | flops 512747520 | bytes 22832640 | tf_op jit(solution)/shard_map/while/body/eval_jaxpr/qhd,khd->hqk/dot_general | solution.py:200
  281.6 8.0 fusion.173
  291.6 8.1 compare_or_fusion.5
  302.1 37.0 %fusion.170 = (f32[12,512]{1,0:T(8,128)S(1)}, f32[12,512,512]{1,2,0:T(8,128)}) fusion(f32[12]{0:T(128)S(1)} %get-tuple-element.1403, pred[512,512]{0,1:T(8,128)(4,1)} %get-tuple-element.1408, f32[12]{0:T(128)S(1)} %get-tuple-element.1409, pred[512,512]{0,1:T(8,128)(4,1)} %get-tuple-element.1410, f32[12]{0:T(128)S(1)} %get-tuple-element.1411, ...), kind=kOutput, calls=%fused_computation.376.clone.1 | convolution fusion | flops 512747520 | bytes 22832640 | tf_op jit(solution)/shard_map/while/body/eval_jaxpr/qhd,khd->hqk/dot_general | solution.py:200
  346.2 8.5 fusion.173
  356.6 8.1 compare_or_fusion.5
  367.1 37.0 %fusion.170 = (f32[12,512]{1,0:T(8,128)S(1)}, f32[12,512,512]{1,2,0:T(8,128)}) fusion(f32[12]{0:T(128)S(1)} %get-tuple-element.1403, pred[512,512]{0,1:T(8,128)(4,1)} %get-tuple-element.1408, f32[12]{0:T(128)S(1)} %get-tuple-element.1409, pred[512,512]{0,1:T(8,128)(4,1)} %get-tuple-element.1410, f32[12]{0:T(128)S(1)} %get-tuple-element.1411, ...), kind=kOutput, calls=%fused_computation.376.clone.1 | convolution fusion | flops 512747520 | bytes 22832640 | tf_op jit(solution)/shard_map/while/body/eval_jaxpr/qhd,khd->hqk/dot_general | solution.py:200
  411.1 8.4 fusion.173
  421.5 8.1 compare_or_fusion.5
  432.0 37.0 %fusion.170 = (f32[12,512]{1,0:T(8,128)S(1)}, f32[12,512,512]{1,2,0:T(8,128)}) fusion(f32[12]{0:T(128)S(1)} %get-tuple-element.1403, pred[512,512]{0,1:T(8,128)(4,1)} %get-tuple-element.1408, f32[12]{0:T(128)S(1)} %get-tuple-element.1409, pred[512,512]{0,1:T(8,128)(4,1)} %get-tuple-element.1410, f32[12]{0:T(128)S(1)} %get-tuple-element.1411, ...), kind=kOutput, calls=%fused_computation.376.clone.1 | convolution fusion | flops 512747520 | bytes 22832640 | tf_op jit(solution)/shard_map/while/body/eval_jaxpr/qhd,khd->hqk/dot_general | solution.py:200
  476.1 8.4 fusion.173
  486.4 8.1 compare_or_fusion.5
  496.9 36.9 %fusion.170 = (f32[12,512]{1,0:T(8,128)S(1)}, f32[12,512,512]{1,2,0:T(8,128)}) fusion(f32[12]{0:T(128)S(1)} %get-tuple-element.1403, pred[512,512]{0,1:T(8,128)(4,1)} %get-tuple-element.1408, f32[12]{0:T(128)S(1)} %get-tuple-element.1409, pred[512,512]{0,1:T(8,128)(4,1)} %get-tuple-element.1410, f32[12]{0:T(128)S(1)} %get-tuple-element.1411, ...), kind=kOutput, calls=%fused_computation.376.clone.1 | convolution fusion | flops 512747520 | bytes 22832640 | tf_op jit(solution)/shard_map/while/body/eval_jaxpr/qhd,khd->hqk/dot_general | solution.py:200
  540.9 8.4 fusion.173
  551.3 8.1 compare_or_fusion.5
  561.8 36.9 %fusion.170 = (f32[12,512]{1,0:T(8,128)S(1)}, f32[12,512,512]{1,2,0:T(8,128)}) fusion(f32[12]{0:T(128)S(1)} %get-tuple-element.1403, pred[512,512]{0,1:T(8,128)(4,1)} %get-tuple-element.1408, f32[12]{0:T(128)S(1)} %get-tuple-element.1409, pred[512,512]{0,1:T(8,128)(4,1)} %get-tuple-element.1410, f32[12]{0:T(128)S(1)} %get-tuple-element.1411, ...), kind=kOutput, calls=%fused_computation.376.clone.1 | convolution fusion | flops 512747520 | bytes 22832640 | tf_op jit(solution)/shard_map/while/body/eval_jaxpr/qhd,khd->hqk/dot_general | solution.py:200
  605.9 8.4 fusion.173
  616.2 8.1 compare_or_fusion.5
  626.7 36.9 %fusion.170 = (f32[12,512]{1,0:T(8,128)S(1)}, f32[12,512,512]{1,2,0:T(8,128)}) fusion(f32[12]{0:T(128)S(1)} %get-tuple-element.1403, pred[512,512]{0,1:T(8,128)(4,1)} %get-tuple-element.1408, f32[12]{0:T(128)S(1)} %get-tuple-element.1409, pred[512,512]{0,1:T(8,128)(4,1)} %get-tuple-element.1410, f32[12]{0:T(128)S(1)} %get-tuple-element.1411, ...), kind=kOutput, calls=%fused_computation.376.clone.1 | convolution fusion | flops 512747520 | bytes 22832640 | tf_op jit(solution)/shard_map/while/body/eval_jaxpr/qhd,khd->hqk/dot_general | solution.py:200
  670.8 8.4 fusion.173
  681.1 8.1 compare_or_fusion.5
  691.6 36.9 %fusion.170 = (f32[12,512]{1,0:T(8,128)S(1)}, f32[12,512,512]{1,2,0:T(8,128)}) fusion(f32[12]{0:T(128)S(1)} %get-tuple-element.1403, pred[512,512]{0,1:T(8,128)(4,1)} %get-tuple-element.1408, f32[12]{0:T(128)S(1)} %get-tuple-element.1409, pred[512,512]{0,1:T(8,128)(4,1)} %get-tuple-element.1410, f32[12]{0:T(128)S(1)} %get-tuple-element.1411, ...), kind=kOutput, calls=%fused_computation.376.clone.1 | convolution fusion | flops 512747520 | bytes 22832640 | tf_op jit(solution)/shard_map/while/body/eval_jaxpr/qhd,khd->hqk/dot_general | solution.py:200
  735.7 8.4 fusion.173
  748.6 9.0 fusion.98
  757.7 10.1 fusion.50
  776.6 8.1 compare_or_fusion.2
  799.9 709.0 %while.47 = (s32[]{:T(128)}, bf16[512,768]{0,1:T(8,128)(2,1)}, bf16[512,768]{0,1:T(8,128)(2,1)}, f32[512,768]{0,1:T(8,128)}, f32[512,768]{0,1:T(8,128)}, /*index...) while((s32[]{:T(128)}, bf16[512,768]{0,1:T(8,128)(2,1)}, ...), condition=%wide.region_13.14_spmd.clone, body=%wide.region_10.13_spmd.clone.sunk | while | flops 2373725440 | bytes 194868528 | solution.py:293
  807.0 8.0 compare_or_fusion.6
  815.0 35.6 %exponential_select_fusion.4 = f32[12,512,512]{2,1,0:T(8,128)S(1)} fusion(f32[12,512]{1,0:T(8,128)S(1)} %get-tuple-element.1653, f32[12]{0:T(128)S(1)} %get-tuple-element.1493, f32[12]{0:T(128)S(1)} %get-tuple-element.1494, f32[12]{0:T(128)S(1)} %get-tuple-element.1495, f32[12]{0:T(128)S(1)} %get-tuple-element.1496, ...), kind=kOutput, calls=%fused_computation.106.clone.1 | convolution fusion | flops 512753664 | bytes 22832640 | tf_op jit(solution)/shard_map/while/body/eval_jaxpr/qhd,khd->hqk/dot_general | solution.py:100
  866.6 14.4 copy.115
  904.8 8.0 compare_or_fusion.6
  912.9 35.8 %exponential_select_fusion.4 = f32[12,512,512]{2,1,0:T(8,128)S(1)} fusion(f32[12,512]{1,0:T(8,128)S(1)} %get-tuple-element.1653, f32[12]{0:T(128)S(1)} %get-tuple-element.1493, f32[12]{0:T(128)S(1)} %get-tuple-element.1494, f32[12]{0:T(128)S(1)} %get-tuple-element.1495, f32[12]{0:T(128)S(1)} %get-tuple-element.1496, ...), kind=kOutput, calls=%fused_computation.106.clone.1 | convolution fusion | flops 512753664 | bytes 22832640 | tf_op jit(solution)/shard_map/while/body/eval_jaxpr/qhd,khd->hqk/dot_general | solution.py:100
  966.0 14.5 copy.115
  986.0 7.7 fusion.191
  1005.9 8.0 compare_or_fusion.6
  1014.0 35.6 %exponential_select_fusion.4 = f32[12,512,512]{2,1,0:T(8,128)S(1)} fusion(f32[12,512]{1,0:T(8,128)S(1)} %get-tuple-element.1653, f32[12]{0:T(128)S(1)} %get-tuple-element.1493, f32[12]{0:T(128)S(1)} %get-tuple-element.1494, f32[12]{0:T(128)S(1)} %get-tuple-element.1495, f32[12]{0:T(128)S(1)} %get-tuple-element.1496, ...), kind=kOutput, calls=%fused_computation.106.clone.1 | convolution fusion | flops 512753664 | bytes 22832640 | tf_op jit(solution)/shard_map/while/body/eval_jaxpr/qhd,khd->hqk/dot_general | solution.py:100
  1065.3 14.4 copy.115
  1104.9 8.0 compare_or_fusion.6
  1113.0 35.6 %exponential_select_fusion.4 = f32[12,512,512]{2,1,0:T(8,128)S(1)} fusion(f32[12,512]{1,0:T(8,128)S(1)} %get-tuple-element.1653, f32[12]{0:T(128)S(1)} %get-tuple-element.1493, f32[12]{0:T(128)S(1)} %get-tuple-element.1494, f32[12]{0:T(128)S(1)} %get-tuple-element.1495, f32[12]{0:T(128)S(1)} %get-tuple-element.1496, ...), kind=kOutput, calls=%fused_computation.106.clone.1 | convolution fusion | flops 512753664 | bytes 22832640 | tf_op jit(solution)/shard_map/while/body/eval_jaxpr/qhd,khd->hqk/dot_general | solution.py:100
  1165.6 14.4 copy.115
  1185.5 7.6 fusion.191
  1205.5 8.0 compare_or_fusion.6
  1213.6 35.6 %exponential_select_fusion.4 = f32[12,512,512]{2,1,0:T(8,128)S(1)} fusion(f32[12,512]{1,0:T(8,128)S(1)} %get-tuple-element.1653, f32[12]{0:T(128)S(1)} %get-tuple-element.1493, f32[12]{0:T(128)S(1)} %get-tuple-element.1494, f32[12]{0:T(128)S(1)} %get-tuple-element.1495, f32[12]{0:T(128)S(1)} %get-tuple-element.1496, ...), kind=kOutput, calls=%fused_computation.106.clone.1 | convolution fusion | flops 512753664 | bytes 22832640 | tf_op jit(solution)/shard_map/while/body/eval_jaxpr/qhd,khd->hqk/dot_general | solution.py:100
  1264.7 14.4 copy.115
  1284.5 7.6 fusion.191
  1304.5 8.0 compare_or_fusion.6
  1312.6 35.6 %exponential_select_fusion.4 = f32[12,512,512]{2,1,0:T(8,128)S(1)} fusion(f32[12,512]{1,0:T(8,128)S(1)} %get-tuple-element.1653, f32[12]{0:T(128)S(1)} %get-tuple-element.1493, f32[12]{0:T(128)S(1)} %get-tuple-element.1494, f32[12]{0:T(128)S(1)} %get-tuple-element.1495, f32[12]{0:T(128)S(1)} %get-tuple-element.1496, ...), kind=kOutput, calls=%fused_computation.106.clone.1 | convolution fusion | flops 512753664 | bytes 22832640 | tf_op jit(solution)/shard_map/while/body/eval_jaxpr/qhd,khd->hqk/dot_general | solution.py:100
  1365.0 14.4 copy.115
  1405.1 8.0 compare_or_fusion.6
  1413.2 35.6 %exponential_select_fusion.4 = f32[12,512,512]{2,1,0:T(8,128)S(1)} fusion(f32[12,512]{1,0:T(8,128)S(1)} %get-tuple-element.1653, f32[12]{0:T(128)S(1)} %get-tuple-element.1493, f32[12]{0:T(128)S(1)} %get-tuple-element.1494, f32[12]{0:T(128)S(1)} %get-tuple-element.1495, f32[12]{0:T(128)S(1)} %get-tuple-element.1496, ...), kind=kOutput, calls=%fused_computation.106.clone.1 | convolution fusion | flops 512753664 | bytes 22832640 | tf_op jit(solution)/shard_map/while/body/eval_jaxpr/qhd,khd->hqk/dot_general | solution.py:100
  1464.1 14.4 copy.115
  1508.9 38.5 %exponential_select_fusion.2 = f32[12,512,512]{2,1,0:T(8,128)} fusion(f32[12,512]{1,0:T(8,128)S(1)} %get-tuple-element.1708, f32[12]{0:T(128)} %get-tuple-element.878, f32[12]{0:T(128)} %get-tuple-element.879, f32[12]{0:T(128)} %get-tuple-element.877, f32[12]{0:T(128)} %get-tuple-element.849, f32[12]{0:T(128)} %get-tuple-element.850, ...), kind=kOutput, calls=%fused_computation.201 | convolution fusion | flops 512753664 | bytes 22832640 | tf_op jit(solution)/shard_map/qhd,khd->hqk/dot_general | solution.py:100
  1567.0 8.6 collective-permute-done.4
  1583.2 8.9 fusion.53
  1595.1 14.7 copy.97
  1626.9 72.6 %reduce-scatter.5.cloned.1.call-done = f32[24,2304]{1,0:T(8,128)} async-done(((f32[768,2304]{1,0:T(8,128)}), f32[24,2304]{1,0:T(8,128)}) %reduce-scatter.5.cloned.1.call-update) | async-done | bytes 221200 | tf_op jit(solution)/shard_map/reduce_scatter | solution.py:309
  1700.6 161.0 %reduce-scatter.9.cloned.1.call-done = f32[24,4096]{1,0:T(8,128)} async-done(((f32[768,4096]{1,0:T(8,128)}), f32[24,4096]{1,0:T(8,128)}) %reduce-scatter.9.cloned.1.call-update) | async-done | bytes 393232 | tf_op jit(solution)/shard_map/reduce_scatter | solution.py:312
  1862.7 41.2 %all-reduce.4 = (f32[768]{0:T(1024)S(1)}, f32[32,12]{0,1:T(8,128)}, f32[768]{0:T(1024)S(1)}, f32[2304]{0:T(1024)S(1)}, f32[768]{0:T(1024)S(1)}, /*index=5*/f32[4096]{0:T(1024)S(1)}, f32[768]{0:T(1024)S(1)}) all-reduce(f32[768]{0:T(1024)S(1)} %get-tuple-element.838, ...), channel_id=2, replica_groups=mesh['batch'=4,'blk'=8] {'batch','blk'}, use_global_device_ids=true, to_apply=%region_18.19.clone | all-reduce | flops 9856 | bytes 78848
  (655 shorter events, 458.7 us)
Async XLA Ops:
  7.2 66.8 %all-gather.7.cloned.1.call-start = ((), (), s32[]{:S(2)}) async-start(), calls=%async_computation.4 | async-start | bytes 3649536 | tf_op jit(solution)/shard_map/all_gather | solution.py:163
  7.9 135.5 %all-gather.9.cloned.1.call-start = ((), (), s32[]{:S(2)}) async-start(), calls=%async_computation.5 | async-start | bytes 7077888 | tf_op jit(solution)/shard_map/all_gather | solution.py:185
  52.0 22.1 %copy-start.41 = (f32[768]{0:T(1024)}, f32[768]{0:T(1024)S(1)}, u32[]{:S(2)}) copy-start(f32[768]{0:T(1024)S(1)} %convert_element_type.4426) | copy-start | bytes 9220
  53.9 20.1 %copy-start.47 = (f32[512]{0:T(512)}, f32[512]{0:T(512)S(1)}, u32[]{:S(2)}) copy-start(f32[512]{0:T(512)S(1)} %fusion.92) | copy-start | bytes 6148
  79.7 129.4 %all-gather.11.cloned.1.call-start = ((), (), s32[]{:S(2)}) async-start(), calls=%async_computation.6 | async-start | bytes 7077888 | tf_op jit(solution)/shard_map/all_gather | solution.py:186
  80.5 665.7 %all-gather.13.cloned.1.call-start = ((), (), s32[]{:S(2)}) async-start(), calls=%async_computation.7 | async-start | bytes 1216512 | tf_op jit(solution)/shard_map/all_gather | solution.py:164
  81.0 667.6 %all-gather.15.cloned.1.call-start = ((), (), s32[]{:S(2)}) async-start(), calls=%async_computation.8 | async-start | bytes 6488064 | tf_op jit(solution)/shard_map/all_gather | solution.py:166
  81.6 676.1 %all-gather.17.cloned.1.call-start = ((), (), s32[]{:S(2)}) async-start(), calls=%async_computation.9 | async-start | bytes 3244032 | tf_op jit(solution)/shard_map/all_gather | solution.py:167
  82.2 1542.6 %reduce-scatter.7.cloned.1.call-start = ((), (), s32[]{:S(2)}) async-start(), calls=%async_computation.11 | async-start | bytes 2433024 | tf_op jit(solution)/shard_map/reduce_scatter | solution.py:310
  85.8 123.3 %copy-start.33 = (s32[512]{0:T(512)}, s32[512]{0:T(512)S(1)}, u32[]{:S(2)}) copy-start(s32[512]{0:T(512)S(1)} %get-tuple-element.1122) | copy-start | bytes 6148
  85.8 123.3 %copy-start.36 = (s32[512]{0:T(512)}, s32[512]{0:T(512)S(1)}, u32[]{:S(2)}) copy-start(s32[512]{0:T(512)S(1)} %get-tuple-element.1123) | copy-start | bytes 6148
  748.5 23.5 %copy-start.16 = (f32[512,768]{1,0:T(8,128)}, f32[512,768]{1,0:T(8,128)S(1)}, u32[]{:S(2)}) copy-start(f32[512,768]{1,0:T(8,128)S(1)} %get-tuple-element.1119) | copy-start | bytes 4718596
  748.6 23.5 %copy-start.31 = (f32[512]{0:T(512)}, f32[512]{0:T(512)S(1)}, u32[]{:S(2)}) copy-start(f32[512]{0:T(512)S(1)} %fusion.93) | copy-start | bytes 6148
  775.9 849.9 %reduce-scatter.11.cloned.1.call-start = ((), (), s32[]{:S(2)}) async-start(), calls=%async_computation.13 | async-start | bytes 6488064 | tf_op jit(solution)/shard_map/reduce_scatter | solution.py:313
  799.8 899.6 %reduce-scatter.5.cloned.1.call-start = ((), (), s32[]{:S(2)}) async-start(), calls=%async_computation.10 | async-start | bytes 7299072 | tf_op jit(solution)/shard_map/reduce_scatter | solution.py:309
  802.9 95.0 %collective-permute-start = (bf16[512,768]{0,1:T(8,128)(2,1)}, bf16[512,768]{0,1:T(8,128)(2,1)}, u32[]{:S(2)}, u32[]{:S(2)}) collective-permute-start(bf16[512,768]{0,1:T(8,128)(2,1)} %copy.139), channel_id=1, source_target_pairs={{0,1},{1,2},{2,3},{3,4},{4,5},{5,6},{6,7},{7,0},{8,9},{9,10},{10,1... | collective-permute-start | bytes 2359304 | tf_op jit(solution)/shard_map/while/body/eval_jaxpr/ppermute | solution.py:20
  805.2 92.7 %collective-permute-start.1 = (bf16[512,768]{0,1:T(8,128)(2,1)}, bf16[512,768]{0,1:T(8,128)(2,1)}, u32[]{:S(2)}, u32[]{:S(2)}) collective-permute-start(bf16[512,768]{0,1:T(8,128)(2,1)} %copy.140), channel_id=1, source_target_pairs={{0,1},{1,2},{2,3},{3,4},{4,5},{5,6},{6,7},{7,0},{8,9},{9,10},{10,1... | collective-permute-start | bytes 2359304 | tf_op jit(solution)/shard_map/while/body/eval_jaxpr/ppermute | solution.py:20
  858.9 33.8 %collective-permute-start.2 = (bf16[512,768]{0,1:T(8,128)(2,1)}, bf16[512,768]{0,1:T(8,128)(2,1)}, u32[]{:S(2)}, u32[]{:S(2)}) collective-permute-start(bf16[512,768]{0,1:T(8,128)(2,1)} %fusion.186), channel_id=1, source_target_pairs={{0,1},{1,2},{2,3},{3,4},{4,5},{5,6},{6,7},{7,0},{8,9},{9,10},{10,1... | collective-permute-start | bytes 2359304 | tf_op jit(solution)/shard_map/while/body/eval_jaxpr/ppermute | solution.py:20
  861.8 33.5 %collective-permute-start.3 = (bf16[512,768]{0,1:T(8,128)(2,1)S(1)}, bf16[512,768]{0,1:T(8,128)(2,1)}, u32[]{:S(2)}, u32[]{:S(2)}) collective-permute-start(bf16[512,768]{0,1:T(8,128)(2,1)S(1)} %fusion.188), channel_id=1, source_target_pairs={{0,1},{1,2},{2,3},{3,4},{4,5},{5,6},{6,7},{7,0},{8,9},{9,10},{10,1... | collective-permute-start | bytes 2359304 | tf_op jit(solution)/shard_map/while/body/eval_jaxpr/ppermute | solution.py:20
  900.6 98.3 %collective-permute-start = (bf16[512,768]{0,1:T(8,128)(2,1)}, bf16[512,768]{0,1:T(8,128)(2,1)}, u32[]{:S(2)}, u32[]{:S(2)}) collective-permute-start(bf16[512,768]{0,1:T(8,128)(2,1)} %copy.139), channel_id=1, source_target_pairs={{0,1},{1,2},{2,3},{3,4},{4,5},{5,6},{6,7},{7,0},{8,9},{9,10},{10,1... | collective-permute-start | bytes 2359304 | tf_op jit(solution)/shard_map/while/body/eval_jaxpr/ppermute | solution.py:20
  902.9 96.0 %collective-permute-start.1 = (bf16[512,768]{0,1:T(8,128)(2,1)}, bf16[512,768]{0,1:T(8,128)(2,1)}, u32[]{:S(2)}, u32[]{:S(2)}) collective-permute-start(bf16[512,768]{0,1:T(8,128)(2,1)} %copy.140), channel_id=1, source_target_pairs={{0,1},{1,2},{2,3},{3,4},{4,5},{5,6},{6,7},{7,0},{8,9},{9,10},{10,1... | collective-permute-start | bytes 2359304 | tf_op jit(solution)/shard_map/while/body/eval_jaxpr/ppermute | solution.py:20
  957.0 36.8 %collective-permute-start.2 = (bf16[512,768]{0,1:T(8,128)(2,1)}, bf16[512,768]{0,1:T(8,128)(2,1)}, u32[]{:S(2)}, u32[]{:S(2)}) collective-permute-start(bf16[512,768]{0,1:T(8,128)(2,1)} %fusion.186), channel_id=1, source_target_pairs={{0,1},{1,2},{2,3},{3,4},{4,5},{5,6},{6,7},{7,0},{8,9},{9,10},{10,1... | collective-permute-start | bytes 2359304 | tf_op jit(solution)/shard_map/while/body/eval_jaxpr/ppermute | solution.py:20
  960.2 36.1 %collective-permute-start.3 = (bf16[512,768]{0,1:T(8,128)(2,1)S(1)}, bf16[512,768]{0,1:T(8,128)(2,1)}, u32[]{:S(2)}, u32[]{:S(2)}) collective-permute-start(bf16[512,768]{0,1:T(8,128)(2,1)S(1)} %fusion.188), channel_id=1, source_target_pairs={{0,1},{1,2},{2,3},{3,4},{4,5},{5,6},{6,7},{7,0},{8,9},{9,10},{10,1... | collective-permute-start | bytes 2359304 | tf_op jit(solution)/shard_map/while/body/eval_jaxpr/ppermute | solution.py:20
  998.9 15.0 copy-start.1
  998.9 15.0 copy-start.4
  1001.6 96.4 %collective-permute-start = (bf16[512,768]{0,1:T(8,128)(2,1)}, bf16[512,768]{0,1:T(8,128)(2,1)}, u32[]{:S(2)}, u32[]{:S(2)}) collective-permute-start(bf16[512,768]{0,1:T(8,128)(2,1)} %copy.139), channel_id=1, source_target_pairs={{0,1},{1,2},{2,3},{3,4},{4,5},{5,6},{6,7},{7,0},{8,9},{9,10},{10,1... | collective-permute-start | bytes 2359304 | tf_op jit(solution)/shard_map/while/body/eval_jaxpr/ppermute | solution.py:20
  1004.0 93.9 %collective-permute-start.1 = (bf16[512,768]{0,1:T(8,128)(2,1)}, bf16[512,768]{0,1:T(8,128)(2,1)}, u32[]{:S(2)}, u32[]{:S(2)}) collective-permute-start(bf16[512,768]{0,1:T(8,128)(2,1)} %copy.140), channel_id=1, source_target_pairs={{0,1},{1,2},{2,3},{3,4},{4,5},{5,6},{6,7},{7,0},{8,9},{9,10},{10,1... | collective-permute-start | bytes 2359304 | tf_op jit(solution)/shard_map/while/body/eval_jaxpr/ppermute | solution.py:20
  1057.8 35.1 %collective-permute-start.2 = (bf16[512,768]{0,1:T(8,128)(2,1)}, bf16[512,768]{0,1:T(8,128)(2,1)}, u32[]{:S(2)}, u32[]{:S(2)}) collective-permute-start(bf16[512,768]{0,1:T(8,128)(2,1)} %fusion.186), channel_id=1, source_target_pairs={{0,1},{1,2},{2,3},{3,4},{4,5},{5,6},{6,7},{7,0},{8,9},{9,10},{10,1... | collective-permute-start | bytes 2359304 | tf_op jit(solution)/shard_map/while/body/eval_jaxpr/ppermute | solution.py:20
  1060.6 34.8 %collective-permute-start.3 = (bf16[512,768]{0,1:T(8,128)(2,1)S(1)}, bf16[512,768]{0,1:T(8,128)(2,1)}, u32[]{:S(2)}, u32[]{:S(2)}) collective-permute-start(bf16[512,768]{0,1:T(8,128)(2,1)S(1)} %fusion.188), channel_id=1, source_target_pairs={{0,1},{1,2},{2,3},{3,4},{4,5},{5,6},{6,7},{7,0},{8,9},{9,10},{10,1... | collective-permute-start | bytes 2359304 | tf_op jit(solution)/shard_map/while/body/eval_jaxpr/ppermute | solution.py:20
  1098.0 15.0 copy-start.1
  1100.6 97.6 %collective-permute-start = (bf16[512,768]{0,1:T(8,128)(2,1)}, bf16[512,768]{0,1:T(8,128)(2,1)}, u32[]{:S(2)}, u32[]{:S(2)}) collective-permute-start(bf16[512,768]{0,1:T(8,128)(2,1)} %copy.139), channel_id=1, source_target_pairs={{0,1},{1,2},{2,3},{3,4},{4,5},{5,6},{6,7},{7,0},{8,9},{9,10},{10,1... | collective-permute-start | bytes 2359304 | tf_op jit(solution)/shard_map/while/body/eval_jaxpr/ppermute | solution.py:20
  1103.1 95.2 %collective-permute-start.1 = (bf16[512,768]{0,1:T(8,128)(2,1)}, bf16[512,768]{0,1:T(8,128)(2,1)}, u32[]{:S(2)}, u32[]{:S(2)}) collective-permute-start(bf16[512,768]{0,1:T(8,128)(2,1)} %copy.140), channel_id=1, source_target_pairs={{0,1},{1,2},{2,3},{3,4},{4,5},{5,6},{6,7},{7,0},{8,9},{9,10},{10,1... | collective-permute-start | bytes 2359304 | tf_op jit(solution)/shard_map/while/body/eval_jaxpr/ppermute | solution.py:20
  1156.8 36.4 %collective-permute-start.2 = (bf16[512,768]{0,1:T(8,128)(2,1)}, bf16[512,768]{0,1:T(8,128)(2,1)}, u32[]{:S(2)}, u32[]{:S(2)}) collective-permute-start(bf16[512,768]{0,1:T(8,128)(2,1)} %fusion.186), channel_id=1, source_target_pairs={{0,1},{1,2},{2,3},{3,4},{4,5},{5,6},{6,7},{7,0},{8,9},{9,10},{10,1... | collective-permute-start | bytes 2359304 | tf_op jit(solution)/shard_map/while/body/eval_jaxpr/ppermute | solution.py:20
  1160.0 35.8 %collective-permute-start.3 = (bf16[512,768]{0,1:T(8,128)(2,1)S(1)}, bf16[512,768]{0,1:T(8,128)(2,1)}, u32[]{:S(2)}, u32[]{:S(2)}) collective-permute-start(bf16[512,768]{0,1:T(8,128)(2,1)S(1)} %fusion.188), channel_id=1, source_target_pairs={{0,1},{1,2},{2,3},{3,4},{4,5},{5,6},{6,7},{7,0},{8,9},{9,10},{10,1... | collective-permute-start | bytes 2359304 | tf_op jit(solution)/shard_map/while/body/eval_jaxpr/ppermute | solution.py:20
  1198.3 15.2 copy-start.1
  1198.3 15.2 copy-start.4
  1201.0 96.4 %collective-permute-start = (bf16[512,768]{0,1:T(8,128)(2,1)}, bf16[512,768]{0,1:T(8,128)(2,1)}, u32[]{:S(2)}, u32[]{:S(2)}) collective-permute-start(bf16[512,768]{0,1:T(8,128)(2,1)} %copy.139), channel_id=1, source_target_pairs={{0,1},{1,2},{2,3},{3,4},{4,5},{5,6},{6,7},{7,0},{8,9},{9,10},{10,1... | collective-permute-start | bytes 2359304 | tf_op jit(solution)/shard_map/while/body/eval_jaxpr/ppermute | solution.py:20
  1203.5 93.8 %collective-permute-start.1 = (bf16[512,768]{0,1:T(8,128)(2,1)}, bf16[512,768]{0,1:T(8,128)(2,1)}, u32[]{:S(2)}, u32[]{:S(2)}) collective-permute-start(bf16[512,768]{0,1:T(8,128)(2,1)} %copy.140), channel_id=1, source_target_pairs={{0,1},{1,2},{2,3},{3,4},{4,5},{5,6},{6,7},{7,0},{8,9},{9,10},{10,1... | collective-permute-start | bytes 2359304 | tf_op jit(solution)/shard_map/while/body/eval_jaxpr/ppermute | solution.py:20
  1257.3 34.9 %collective-permute-start.2 = (bf16[512,768]{0,1:T(8,128)(2,1)}, bf16[512,768]{0,1:T(8,128)(2,1)}, u32[]{:S(2)}, u32[]{:S(2)}) collective-permute-start(bf16[512,768]{0,1:T(8,128)(2,1)} %fusion.186), channel_id=1, source_target_pairs={{0,1},{1,2},{2,3},{3,4},{4,5},{5,6},{6,7},{7,0},{8,9},{9,10},{10,1... | collective-permute-start | bytes 2359304 | tf_op jit(solution)/shard_map/while/body/eval_jaxpr/ppermute | solution.py:20
  1260.3 34.5 %collective-permute-start.3 = (bf16[512,768]{0,1:T(8,128)(2,1)S(1)}, bf16[512,768]{0,1:T(8,128)(2,1)}, u32[]{:S(2)}, u32[]{:S(2)}) collective-permute-start(bf16[512,768]{0,1:T(8,128)(2,1)S(1)} %fusion.188), channel_id=1, source_target_pairs={{0,1},{1,2},{2,3},{3,4},{4,5},{5,6},{6,7},{7,0},{8,9},{9,10},{10,1... | collective-permute-start | bytes 2359304 | tf_op jit(solution)/shard_map/while/body/eval_jaxpr/ppermute | solution.py:20
  1297.4 15.2 copy-start.1
  1297.4 15.2 copy-start.4
  1300.0 97.6 %collective-permute-start = (bf16[512,768]{0,1:T(8,128)(2,1)}, bf16[512,768]{0,1:T(8,128)(2,1)}, u32[]{:S(2)}, u32[]{:S(2)}) collective-permute-start(bf16[512,768]{0,1:T(8,128)(2,1)} %copy.139), channel_id=1, source_target_pairs={{0,1},{1,2},{2,3},{3,4},{4,5},{5,6},{6,7},{7,0},{8,9},{9,10},{10,1... | collective-permute-start | bytes 2359304 | tf_op jit(solution)/shard_map/while/body/eval_jaxpr/ppermute | solution.py:20
  1302.6 95.1 %collective-permute-start.1 = (bf16[512,768]{0,1:T(8,128)(2,1)}, bf16[512,768]{0,1:T(8,128)(2,1)}, u32[]{:S(2)}, u32[]{:S(2)}) collective-permute-start(bf16[512,768]{0,1:T(8,128)(2,1)} %copy.140), channel_id=1, source_target_pairs={{0,1},{1,2},{2,3},{3,4},{4,5},{5,6},{6,7},{7,0},{8,9},{9,10},{10,1... | collective-permute-start | bytes 2359304 | tf_op jit(solution)/shard_map/while/body/eval_jaxpr/ppermute | solution.py:20
  1356.4 36.2 %collective-permute-start.2 = (bf16[512,768]{0,1:T(8,128)(2,1)}, bf16[512,768]{0,1:T(8,128)(2,1)}, u32[]{:S(2)}, u32[]{:S(2)}) collective-permute-start(bf16[512,768]{0,1:T(8,128)(2,1)} %fusion.186), channel_id=1, source_target_pairs={{0,1},{1,2},{2,3},{3,4},{4,5},{5,6},{6,7},{7,0},{8,9},{9,10},{10,1... | collective-permute-start | bytes 2359304 | tf_op jit(solution)/shard_map/while/body/eval_jaxpr/ppermute | solution.py:20
  1359.6 35.5 %collective-permute-start.3 = (bf16[512,768]{0,1:T(8,128)(2,1)S(1)}, bf16[512,768]{0,1:T(8,128)(2,1)}, u32[]{:S(2)}, u32[]{:S(2)}) collective-permute-start(bf16[512,768]{0,1:T(8,128)(2,1)S(1)} %fusion.188), channel_id=1, source_target_pairs={{0,1},{1,2},{2,3},{3,4},{4,5},{5,6},{6,7},{7,0},{8,9},{9,10},{10,1... | collective-permute-start | bytes 2359304 | tf_op jit(solution)/shard_map/while/body/eval_jaxpr/ppermute | solution.py:20
  1397.7 15.5 copy-start.1
  1397.7 15.5 copy-start.4
  1400.4 96.4 %collective-permute-start = (bf16[512,768]{0,1:T(8,128)(2,1)}, bf16[512,768]{0,1:T(8,128)(2,1)}, u32[]{:S(2)}, u32[]{:S(2)}) collective-permute-start(bf16[512,768]{0,1:T(8,128)(2,1)} %copy.139), channel_id=1, source_target_pairs={{0,1},{1,2},{2,3},{3,4},{4,5},{5,6},{6,7},{7,0},{8,9},{9,10},{10,1... | collective-permute-start | bytes 2359304 | tf_op jit(solution)/shard_map/while/body/eval_jaxpr/ppermute | solution.py:20
  1402.9 93.8 %collective-permute-start.1 = (bf16[512,768]{0,1:T(8,128)(2,1)}, bf16[512,768]{0,1:T(8,128)(2,1)}, u32[]{:S(2)}, u32[]{:S(2)}) collective-permute-start(bf16[512,768]{0,1:T(8,128)(2,1)} %copy.140), channel_id=1, source_target_pairs={{0,1},{1,2},{2,3},{3,4},{4,5},{5,6},{6,7},{7,0},{8,9},{9,10},{10,1... | collective-permute-start | bytes 2359304 | tf_op jit(solution)/shard_map/while/body/eval_jaxpr/ppermute | solution.py:20
  1457.0 34.6 %collective-permute-start.2 = (bf16[512,768]{0,1:T(8,128)(2,1)}, bf16[512,768]{0,1:T(8,128)(2,1)}, u32[]{:S(2)}, u32[]{:S(2)}) collective-permute-start(bf16[512,768]{0,1:T(8,128)(2,1)} %fusion.186), channel_id=1, source_target_pairs={{0,1},{1,2},{2,3},{3,4},{4,5},{5,6},{6,7},{7,0},{8,9},{9,10},{10,1... | collective-permute-start | bytes 2359304 | tf_op jit(solution)/shard_map/while/body/eval_jaxpr/ppermute | solution.py:20
  1459.9 34.3 %collective-permute-start.3 = (bf16[512,768]{0,1:T(8,128)(2,1)S(1)}, bf16[512,768]{0,1:T(8,128)(2,1)}, u32[]{:S(2)}, u32[]{:S(2)}) collective-permute-start(bf16[512,768]{0,1:T(8,128)(2,1)S(1)} %fusion.188), channel_id=1, source_target_pairs={{0,1},{1,2},{2,3},{3,4},{4,5},{5,6},{6,7},{7,0},{8,9},{9,10},{10,1... | collective-permute-start | bytes 2359304 | tf_op jit(solution)/shard_map/while/body/eval_jaxpr/ppermute | solution.py:20
  1553.8 13.3 collective-permute-start.5
  1562.4 13.3 collective-permute-start.4
  1581.8 279.8 %reduce-scatter.9.cloned.1.call-start = ((), (), s32[]{:S(2)}) async-start(), calls=%async_computation.12 | async-start | bytes 12976128 | tf_op jit(solution)/shard_map/reduce_scatter | solution.py:312
  1623.3 239.4 %copy-start.51 = (f32[768]{0:T(1024)S(1)}, f32[768]{0:T(1024)}, u32[]{:S(2)}) copy-start(f32[768]{0:T(1024)} %get-tuple-element.836) | copy-start | bytes 9220
  1623.3 286.8 %copy-start.44 = (f32[2304]{0:T(1024)S(1)}, f32[2304]{0:T(1024)}, u32[]{:S(2)}) copy-start(f32[2304]{0:T(1024)} %param.33) | copy-start | bytes 27652
  1623.4 287.4 %copy-start.52 = (f32[24]{0:T(128)S(1)}, f32[24]{0:T(128)}, u32[]{:S(2)}) copy-start(f32[24]{0:T(128)} %param.32) | copy-start | bytes 292
  1623.4 287.9 %copy-start.49 = (f32[768]{0:T(1024)S(1)}, f32[768]{0:T(1024)}, u32[]{:S(2)}) copy-start(f32[768]{0:T(1024)} %param.35) | copy-start | bytes 9220
  1623.4 288.5 %copy-start.53 = (f32[24]{0:T(128)S(1)}, f32[24]{0:T(128)}, u32[]{:S(2)}) copy-start(f32[24]{0:T(128)} %param.34) | copy-start | bytes 292
  1623.4 289.0 %copy-start.43 = (f32[4096]{0:T(1024)S(1)}, f32[4096]{0:T(1024)}, u32[]{:S(2)}) copy-start(f32[4096]{0:T(1024)} %param.37) | copy-start | bytes 49156
  1623.4 289.6 %copy-start.54 = (f32[24]{0:T(128)S(1)}, f32[24]{0:T(128)}, u32[]{:S(2)}) copy-start(f32[24]{0:T(128)} %param.36) | copy-start | bytes 292
  1623.4 290.1 %copy-start.50 = (f32[768]{0:T(1024)S(1)}, f32[768]{0:T(1024)}, u32[]{:S(2)}) copy-start(f32[768]{0:T(1024)} %param.39) | copy-start | bytes 9220
  1623.4 290.7 %copy-start.55 = (f32[64]{0:T(128)S(1)}, f32[64]{0:T(128)}, u32[]{:S(2)}) copy-start(f32[64]{0:T(128)} %param.38) | copy-start | bytes 772
  (101 other events, 552.9 us)
Sparse Core Ops, SparseCore 0:
  11.0 62.9 all-gather.6
  79.8 63.5 all-gather.8
  145.6 63.3 all-gather.10
  212.0 52.8 all-gather.12
  267.7 68.3 all-gather.14
  338.9 57.6 all-gather.16
  776.0 107.1 reduce-scatter.6
  890.4 116.0 reduce-scatter.10
  1581.9 117.5 reduce-scatter.4
  1707.0 154.5 reduce-scatter.8
where the time goes:
time: 1930 us; the launch traced here: 1920 us
  matrix products  872 us (45%)
  waiting for transfers between devices  388 us (20%)
  other arithmetic  290 us (15%)
  local copies, waits for them, and re-layouts  221 us (11%)
  blocking collectives  83.5 us (4%)
  loops' own time  30.6 us (2%)
  starting transfers between devices  19.3 us (1%)
    dot_general x8, matrix products, one_block(): jnp.einsum('qhd,khd->hqk', query3, key_block, preferred_element_type=jnp....  296 us
    dot_general x8, matrix products, pair_grads(): jnp.einsum('qhd,khd->hqk', query3, key3, preferred_element_type=jnp.float32)  288 us
    reduce_scatter x1, waiting for transfers between devices, shards(): lax.psum_scatter(grad_gateup, ('batch', 'blk'), scatter_dimension=0, tile...  161 us
    or x16, other arithmetic, pair_layout(): (query_seg[:, None] == key_seg[None, :]) & ~key_pad[None, :]  129 us
    convert_element_type x8, local copies, waits for them, and re-layouts, pair_grads(): dscores = (weights * (dprob - delta[:, :, None])).astype(jnp.bfloat16)  116 us
    unnamed x2, blocking collectives  83.5 us
    reduce_scatter x1, waiting for transfers between devices, shards(): lax.psum_scatter(grad_qkv, ('batch', 'blk'), scatter_dimension=0, tiled=T...  72.6 us
    dot_general x8, matrix products, one_block(): jnp.einsum('hqk,khd->hqd', unnorm.astype(jnp.bfloat16), value_block, pref...  67.1 us
  transfers between devices with their start and end apart: 40, of which 7 were waited for; matrix products, arithmetic and copies ran while one was open for 70% of the time, Pallas kernels for 0%

commit v1 on v0

v1 whole, which is shorter than its diff:
```python
import functools
import math

import jax
import jax.numpy as jnp
from jax import lax
from jax.experimental import pallas as pl
from jax.experimental.pallas import tpu as pltpu
from jax.sharding import PartitionSpec as P

THRESHOLDS = (12, 16, 23, 32, 46, 64, 91)
EPSILON = 1e-06
DECAY_RATE = 0.5
GELU_SCALE = 0.7978845608028654
MASKED = -1e9
ALL = ("batch", "blk")
LANES = 128
TILE = 256
GROUP = 4
VMEM = 56 * 2**20
F32 = jnp.float32
BF16 = jnp.bfloat16


def bucket_of(offset):
    distance = jnp.abs(offset)
    steps_up = 8 + sum(((distance >= limit).astype(jnp.int32) for limit in THRESHOLDS))
    within = jnp.where(distance < 8, distance, steps_up)
    return within + 16 * (offset > 0).astype(jnp.int32)


def rms_scale(values, gain):
    return values * lax.rsqrt(jnp.mean(values * values, axis=-1, keepdims=True) + EPSILON) * gain


def rms_back(values, gain, grad):
    scale = lax.rsqrt(jnp.mean(values * values, axis=-1, keepdims=True) + EPSILON)
    scaled = grad * gain
    return scale * scaled - values * scale**3 * jnp.mean(scaled * values, axis=-1, keepdims=True)


def gelu_tanh(values):
    return (
        0.5 * values * (1.0 + jnp.tanh(GELU_SCALE * (values + 0.044715 * values * values * values)))
    )


def gated(gate, upward):
    return gelu_tanh(gate) * upward


def dot_nn(left, right):
    return jnp.dot(left, right, preferred_element_type=F32)


def dot_tn(left, right):
    return lax.dot_general(left, right, (((0,), (0,)), ((), ())), preferred_element_type=F32)


def dot_nt(left, right):
    return lax.dot_general(left, right, (((1,), (1,)), ((), ())), preferred_element_type=F32)


def dot_tt(left, right):
    return lax.dot_general(left, right, (((0,), (1,)), ((), ())), preferred_element_type=F32)


class Layout:
    def __init__(self, tokens, groups, splits, ints):
        self.tokens, self.groups, self.splits = tokens, groups, splits
        self.blocks = groups * splits
        self.seq = tokens * self.blocks
        self.near = tokens + 2 * LANES
        self.subs = tokens // LANES
        self.group, self.split = ints[0], ints[1]
        self.ends = (ints[2], ints[3], ints[4])
        slot = pl.program_id(0)
        self.block = self.block_of(slot, 0)
        self.first = pl.multiple_of(self.block * tokens, LANES)
        self.lefts = jnp.maximum(0, self.block * (tokens // TILE) - 1)
        self.loops = (self.seq // TILE - 2 - tokens // TILE) // GROUP
        self.edge = jnp.logical_or(self.block == 0, self.block == self.blocks - 1)

    def block_of(self, slot, other):
        return lax.rem(self.group - slot + self.groups, self.groups) * self.splits + lax.rem(
            self.split + other, self.splits
        )

    def keys_of(self, tile):
        before = 2 * LANES + TILE * tile
        after = self.first + self.near + TILE * (tile - self.lefts)
        return pl.ds(pl.multiple_of(jnp.where(tile < self.lefts, before, after), LANES), TILE)

    def rows_of(self, tile):
        return pl.ds(pl.multiple_of(self.near + TILE * tile, LANES), TILE)

    def segment(self, positions):
        return sum((positions >= end).astype(jnp.int32) for end in self.ends)


def iota(shape, dim):
    return lax.broadcasted_iota(jnp.int32, shape, dim)


def fold(values):
    return values.reshape(values.shape[0] // 8, 8, values.shape[1])


def forward_kernel(tokens, groups, splits, ints, table, query, *refs):
    kvs, (probs, context, stats, k_aug, v_t, scores, biases, best) = refs[:splits], refs[splits:]
    lay = Layout(tokens, groups, splits, ints)
    half = query.shape[1] // 2
    buckets = table.shape[1]

    @pl.when(pl.program_id(0) == 0)
    def prepare():
        lane = iota((tokens, LANES), 1)
        for slot in range(groups):
            for other in range(splits):
                start = lay.block_of(slot, other) * tokens
                rows = pl.ds(pl.multiple_of(LANES + start, LANES), tokens)
                kv = kvs[other][slot * tokens : (slot + 1) * tokens, :].astype(F32)
                seg = lay.segment(start + iota((tokens, LANES), 0))
                k_aug[rows, :] = jnp.where(lane < half, kv, (lane - half == seg).astype(F32)).astype(BF16)
                turned = jnp.transpose(kv)
                ones = (iota((16, tokens), 0) == 0).astype(F32)
                v_t[:, rows] = jnp.concatenate([turned[half:], ones], axis=0).astype(BF16)
        outside = (iota((LANES, LANES), 1) == half + 3).astype(BF16)
        for start in (0, lay.seq + LANES):
            k_aug[start : start + LANES, :] = outside
            v_t[:, start : start + LANES] = jnp.zeros((half + 16, LANES), BF16)
        for place in range(3):
            bucket = bucket_of(
                LANES * (place - 1) + iota((LANES, LANES), 0) - iota((LANES, LANES), 1)
            )
            bias = jnp.zeros((LANES, LANES), F32)
            for label in range(buckets):
                bias = jnp.where(bucket == label, table[0, label], bias)
            biases[place] = bias

    far_left, far_right = table[0, buckets // 2 - 1], table[0, buckets - 1]
    positions = lay.block * tokens + iota((1, tokens), 1)
    seg_q = lay.segment(positions)
    row = iota((2 * half, tokens), 0)
    apart = jnp.logical_or(row - half != seg_q, row == half + 3)
    q_aug = jnp.where(
        row < half, jnp.transpose(query[...].astype(F32)), jnp.where(apart, MASKED, 0.0)
    ).astype(BF16)

    near = dot_nn(k_aug[pl.ds(lay.first, lay.near), :], q_aug)
    eye = iota((LANES, LANES), 0) == iota((LANES, LANES), 1)
    for sub_q in range(lay.subs):
        lanes = slice(LANES * sub_q, LANES * (sub_q + 1))
        top = None
        for sub_k in range(lay.subs + 2):
            rows = slice(LANES * sub_k, LANES * (sub_k + 1))
            place = sub_k - sub_q
            piece = near[rows, lanes] + (
                far_left if place < 0 else far_right if place > 2 else biases[place]
            )
            if place == 1:
                alone = jnp.logical_and(eye, positions[:, lanes] >= lay.ends[2])
                piece = jnp.where(alone, 0.0, piece)
            scores[rows, lanes] = piece
            high = jnp.max(fold(piece), axis=0)
            top = high if top is None else jnp.maximum(top, high)
        best[:, lanes] = top

    def score(tile):
        piece = dot_nn(k_aug[lay.keys_of(tile), :], q_aug)
        scores[lay.rows_of(tile), :] = piece
        const = jnp.where(tile < lay.lefts, far_left, far_right)
        return jnp.max(fold(piece), axis=0) + const

    def score_group(index, top):
        for step in range(GROUP):
            top = jnp.maximum(top, score(index * GROUP + step))
        return top

    best[...] = lax.fori_loop(0, lay.loops, score_group, best[...])

    @pl.when(lay.edge)
    def _():
        best[...] = jnp.maximum(best[...], score(lay.loops * GROUP))

    peak = jnp.max(best[...], axis=0, keepdims=True)
    weights = jnp.exp(scores[: lay.near, :] - peak).astype(BF16)
    probs[: lay.near, :] = weights
    total = dot_nn(v_t[:, pl.ds(lay.first, lay.near)], weights)

    def weigh(tile):
        const = jnp.where(tile < lay.lefts, far_left, far_right)
        rows = lay.rows_of(tile)
        part = jnp.exp(scores[rows, :] - (peak - const)).astype(BF16)
        probs[rows, :] = part
        return dot_nn(v_t[:, lay.keys_of(tile)], part)

    def weigh_group(index, total):
        return total + sum(weigh(index * GROUP + step) for step in range(GROUP))

    stats[...] = lax.fori_loop(0, lay.loops, weigh_group, total)

    @pl.when(lay.edge)
    def _():
        stats[...] += weigh(lay.loops * GROUP)

    inverse = 1.0 / stats[half : half + 1, :]
    result = stats[:half, :] * inverse
    context[...] = result.astype(BF16)
    stats[:half, :] = result
    stats[half : half + 1, :] = inverse


def backward_kernel(tokens, groups, splits, ints, query, d_context, stats, probs, *refs):
    kvs, d_query, d_kvs = refs[:splits], refs[splits], refs[splits + 1 : 2 * splits + 1]
    d_table, v_aug, k_t, d_kv, bands, sides, d_q = refs[2 * splits + 1 :]
    lay = Layout(tokens, groups, splits, ints)
    half = query.shape[1] // 2
    buckets = d_table.shape[0]

    @pl.when(pl.program_id(0) == 0)
    def prepare():
        lane = iota((tokens, LANES), 1)
        for slot in range(groups):
            for other in range(splits):
                start = lay.block_of(slot, other) * tokens
                rows = pl.ds(pl.multiple_of(LANES + start, LANES), tokens)
                kv = kvs[other][slot * tokens : (slot + 1) * tokens, :].astype(F32)
                v_aug[rows, :] = jnp.where(lane >= half, kv, (lane < 3).astype(F32)).astype(BF16)
                ones = (iota((16, tokens), 0) == 0).astype(F32)
                k_t[:, rows] = jnp.concatenate([jnp.transpose(kv)[:half], ones], axis=0).astype(BF16)
        for start in (0, lay.seq + LANES):
            v_aug[start : start + LANES, :] = jnp.zeros((LANES, LANES), BF16)
            k_t[:, start : start + LANES] = jnp.zeros((half + 16, LANES), BF16)
        d_kv[...] = jnp.zeros_like(d_kv)
        bands[...] = jnp.zeros_like(bands)
        sides[...] = jnp.zeros_like(sides)

    inverse = stats[half : half + 1, :]
    upstream = d_context[...].astype(F32)
    delta = jnp.sum(upstream * stats[:half, :], axis=0, keepdims=True) * inverse
    scaled = upstream * inverse
    high = delta.astype(BF16).astype(F32)
    middle = (delta - high).astype(BF16).astype(F32)
    low = delta - high - middle
    row = iota((half, tokens), 0)
    shift = jnp.where(row == 0, high, jnp.where(row == 1, middle, jnp.where(row == 2, low, 0.0)))
    up_aug = jnp.concatenate([-shift, scaled], axis=0).astype(BF16)
    up_rows = jnp.transpose(jnp.concatenate([jnp.zeros_like(scaled), scaled], axis=0)).astype(BF16)
    both = jnp.concatenate([query[...], up_rows], axis=0)

    def grads(keys, rows):
        part = probs[rows, :]
        d_scores = part.astype(F32) * dot_nn(v_aug[keys, :], up_aug)
        rounded = d_scores.astype(BF16)
        d_kv[keys, :] += dot_nn(jnp.concatenate([rounded, part], axis=1), both)
        return d_scores, dot_nn(k_t[:, keys], rounded)

    near, total = grads(pl.ds(lay.first, lay.near), pl.ds(0, lay.near))
    for sub_q in range(lay.subs):
        lanes = slice(LANES * sub_q, LANES * (sub_q + 1))
        for sub_k in range(lay.subs + 2):
            piece = near[LANES * sub_k : LANES * (sub_k + 1), lanes]
            place = sub_k - sub_q
            if 0 <= place <= 2:
                bands[place] += piece
            else:
                sides[int(place > 2), :, lanes] += jnp.sum(fold(piece), axis=0)
    d_q[...] = total
    near_sum = total[half : half + 8, :]

    def far(tile):
        part = grads(lay.keys_of(tile), lay.rows_of(tile))[1]
        return part, jnp.where(tile < lay.lefts, part[half : half + 8, :], 0.0)

    def far_group(index, left):
        parts = [far(index * GROUP + step) for step in range(GROUP)]
        d_q[...] += sum(part for part, _ in parts)
        return left + sum(side for _, side in parts)

    left_sum = lax.fori_loop(0, lay.loops, far_group, jnp.zeros((8, tokens), F32))
    sides[0] += left_sum

    @pl.when(lay.edge)
    def _():
        part, side = far(lay.loops * GROUP)
        d_q[...] += part
        sides[0] += side
        sides[1] -= side

    sides[1] += d_q[half : half + 8, :] - near_sum - left_sum
    d_query[...] = d_q[:half, :].astype(BF16)

    @pl.when(pl.program_id(0) == groups - 1)
    def finish():
        for slot in range(groups):
            for other in range(splits):
                start = lay.block_of(slot, other) * tokens
                rows = pl.ds(pl.multiple_of(LANES + start, LANES), tokens)
                d_kvs[other][slot * tokens : (slot + 1) * tokens, :] = d_kv[rows, :].astype(BF16)
        labels = [
            bucket_of(LANES * (place - 1) + iota((LANES, LANES), 0) - iota((LANES, LANES), 1))
            for place in range(3)
        ]
        for label in range(buckets):
            found = jnp.zeros((8, LANES), F32)
            for place in range(3):
                kept = jnp.where(labels[place] == label, bands[place], 0.0)
                found += jnp.sum(fold(kept), axis=0)
            if label in (buckets // 2 - 1, buckets - 1):
                side = sides[int(label == buckets - 1)]
                for sub in range(lay.subs):
                    found += side[:, LANES * sub : LANES * (sub + 1)]
            d_table[label : label + 1, :] = jnp.sum(found, axis=0, keepdims=True)


def smem():
    return pl.BlockSpec(memory_space=pltpu.SMEM)


def attend(head, tokens, groups, splits, ints, table, query, kvs):
    seq, rows = tokens * groups * splits, tokens * groups
    half = LANES // 2
    column = lambda slot: (0, slot)
    whole = pl.BlockSpec((rows, LANES), lambda slot: (0, head))
    return pl.pallas_call(
        functools.partial(forward_kernel, tokens, groups, splits),
        grid=(groups,),
        in_specs=[smem(), smem(), pl.BlockSpec((tokens, LANES), lambda slot: (slot, head))]
        + [whole] * splits,
        out_specs=[
            pl.BlockSpec((seq, tokens), lambda slot: (slot, 0)),
            pl.BlockSpec((half, tokens), column),
            pl.BlockSpec((half + 16, tokens), column),
        ],
        out_shape=[
            jax.ShapeDtypeStruct((groups * seq, tokens), BF16),
            jax.ShapeDtypeStruct((half, rows), BF16),
            jax.ShapeDtypeStruct((half + 16, rows), F32),
        ],
        scratch_shapes=[
            pltpu.VMEM((seq + 2 * LANES, LANES), BF16),
            pltpu.VMEM((half + 16, seq + 2 * LANES), BF16),
            pltpu.VMEM((seq, tokens), F32),
            pltpu.VMEM((3, LANES, LANES), F32),
            pltpu.VMEM((8, tokens), F32),
        ],
        compiler_params=pltpu.CompilerParams(vmem_limit_bytes=VMEM),
        cost_estimate=pl.CostEstimate(
            flops=16 * seq * rows * half, bytes_accessed=2 * seq * rows, transcendentals=seq * rows
        ),
        name="attend",
    )(ints, table, query, *kvs)


def attend_back(head, tokens, groups, splits, ints, buckets, query, d_context, stats, probs, kvs):
    seq, rows = tokens * groups * splits, tokens * groups
    half = LANES // 2
    column = lambda slot: (0, slot)
    whole = pl.BlockSpec((rows, LANES), lambda slot: (0, head))
    kept = pl.BlockSpec((rows, LANES), lambda slot: (0, 0))
    return pl.pallas_call(
        functools.partial(backward_kernel, tokens, groups, splits),
        grid=(groups,),
        in_specs=[
            smem(),
            pl.BlockSpec((tokens, LANES), lambda slot: (slot, head)),
            pl.BlockSpec((half, tokens), column),
            pl.BlockSpec((half + 16, tokens), column),
            pl.BlockSpec((seq, tokens), lambda slot: (slot, 0)),
        ]
        + [whole] * splits,
        out_specs=[pl.BlockSpec((half, tokens), column)]
        + [kept] * splits
        + [pl.BlockSpec((buckets, LANES), lambda slot: (0, 0))],
        out_shape=[jax.ShapeDtypeStruct((half, rows), BF16)]
        + [jax.ShapeDtypeStruct((rows, LANES), BF16)] * splits
        + [jax.ShapeDtypeStruct((buckets, LANES), F32)],
        scratch_shapes=[
            pltpu.VMEM((seq + 2 * LANES, LANES), BF16),
            pltpu.VMEM((half + 16, seq + 2 * LANES), BF16),
            pltpu.VMEM((seq + 2 * LANES, LANES), F32),
            pltpu.VMEM((3, LANES, LANES), F32),
            pltpu.VMEM((2, 8, tokens), F32),
            pltpu.VMEM((half + 16, tokens), F32),
        ],
        compiler_params=pltpu.CompilerParams(vmem_limit_bytes=VMEM),
        cost_estimate=pl.CostEstimate(
            flops=32 * seq * rows * half, bytes_accessed=2 * seq * rows, transcendentals=0
        ),
        name="attend_back",
    )(ints, query, d_context, stats, probs, *kvs)


def factored(grad_shard, column_total, row_old, column_old, row_total):
    columns = grad_shard.shape[1]
    mean_square = jnp.sum(column_total) / (row_total * columns) + EPSILON
    row_new = (
        DECAY_RATE * row_old
        + (1.0 - DECAY_RATE) * (jnp.sum(grad_shard * grad_shard, axis=1) / columns) / mean_square
    )
    column_new = (
        DECAY_RATE * column_old + (1.0 - DECAY_RATE) * (column_total / row_total) / mean_square
    )
    return (row_new, column_new)


def rolled(array, axis, by):
    size = array.shape[axis]
    return lax.dynamic_slice_in_dim(jnp.concatenate([array, array], axis=axis), by, size, axis)


def shards(
    tokens,
    lengths,
    norm_one,
    w_qkv,
    rel_table,
    w_out,
    norm_two,
    w_gateup,
    w_down,
    cotangent,
    row_qkv,
    col_qkv,
    row_out,
    col_out,
    row_gateup,
    col_gateup,
    row_down,
    col_down,
):
    own = tokens[0]
    tok_rows, width = own.shape
    heads = rel_table.shape[1]
    buckets = rel_table.shape[0]
    ring = lax.axis_size("blk")
    rows_apart = lax.axis_size("batch")
    groups = math.gcd(ring, heads)
    splits = ring // groups
    group_heads = heads // groups
    place = lax.axis_index("blk")
    group, split = place // splits, place % splits
    batch = lax.axis_index("batch")
    group_width = width // groups

    def line(array, by):
        step = by * splits
        return lax.ppermute(
            array, "blk", [(i, i + step) for i in range(ring) if 0 <= i + step < ring]
        )

    def from_group(array, ahead):
        step = ahead * splits
        return lax.ppermute(array, "blk", [(i, (i - step) % ring) for i in range(ring)])

    def from_split(array, ahead):
        pairs = []
        for i in range(ring):
            base = i // splits * splits
            pairs.append((base + (i - base + ahead) % splits, i))
        return lax.ppermute(array, "blk", pairs)

    ahead, behind = [own], [own]
    for _ in range(groups - 1):
        ahead.append(line(ahead[-1], 1))
        behind.append(line(behind[-1], -1))
    gathered = [own] + [ahead[s] + behind[groups - s] for s in range(1, groups)]

    gains = jnp.pad(jnp.stack([norm_one, norm_two], axis=1), ((0, 0), (0, LANES - 2)))
    full_qkv = lax.all_gather(jnp.concatenate([w_qkv, gains], axis=1), ALL, axis=0, tiled=True)
    full_out = lax.all_gather(w_out, ALL, axis=0, tiled=True)
    full_gateup = lax.all_gather(w_gateup, ALL, axis=0, tiled=True)
    full_down = lax.all_gather(w_down, ALL, axis=0, tiled=True)
    gain_one = full_qkv[:, 3 * width].astype(F32)
    gain_two = full_qkv[:, 3 * width + 1].astype(F32)

    split_qkv = rolled(
        full_qkv[:, : 3 * width].reshape(width, 3, groups, group_width), 2, group
    ).reshape(width, 3, groups, group_heads, LANES // 2)
    w_query = split_qkv[:, 0].reshape(width, width)
    w_kv = jnp.moveaxis(split_qkv[:, 1:], 1, 3).reshape(width, 2 * width)
    out_rel = rolled(full_out, 0, group * group_width)
    w_query_own = jnp.pad(
        split_qkv[:, 0, 0], ((0, 0), (0, 0), (0, LANES // 2))
    ).reshape(width, group_heads * LANES)

    normed = rms_scale(
        jnp.concatenate(gathered, axis=0).astype(F32), gain_one
    ).astype(BF16)
    query = dot_nn(normed, w_query_own).astype(BF16)
    kv = dot_nn(normed, w_kv[:, : 2 * group_width]).astype(BF16)
    kvs = [kv] + [from_split(kv, other) for other in range(1, splits)]

    ends = jnp.cumsum(lengths[0])
    ints = jnp.concatenate([jnp.stack([group, split]).astype(jnp.int32), ends.astype(jnp.int32)])
    table_own = lax.dynamic_slice_in_dim(rel_table.T, group * group_heads, group_heads, 0)

    contexts, stats, probs = [], [], []
    for head in range(group_heads):
        prob, context, stat = attend(
            head, tok_rows, groups, splits, ints, table_own[head : head + 1], query, kvs
        )
        contexts.append(context)
        stats.append(stat)
        probs.append(prob)

    def slot_of(array, slot, axis):
        return lax.slice_in_dim(array, slot * tok_rows, (slot + 1) * tok_rows, axis=axis)

    context_t = jnp.concatenate(
        [
            from_group(slot_of(contexts[head], s, 1), s) if s else slot_of(contexts[head], 0, 1)
            for s in range(groups)
            for head in range(group_heads)
        ],
        axis=0,
    )

    inputs = own.astype(F32)
    mixed = inputs + dot_tn(context_t, out_rel)
    normed_two = rms_scale(mixed, gain_two).astype(BF16)
    gate_up = dot_nn(normed_two, full_gateup)
    hidden_units = gate_up.shape[1] // 2
    gate = gate_up[:, :hidden_units]
    upward = gate_up[:, hidden_units:]
    hidden = gated(gate, upward).astype(BF16)
    result = (mixed + dot_nn(hidden, full_down)).astype(BF16)
    upstream = cotangent[0]
    d_hidden = dot_nt(upstream, full_down)
    grad_down = dot_tn(hidden, upstream)
    d_gate, d_upward = jax.vjp(gated, gate, upward)[1](d_hidden)
    grad_act = jnp.concatenate([d_gate, d_upward], axis=1).astype(BF16)
    grad_gateup = dot_tn(normed_two, grad_act)
    d_normed_two = dot_nt(grad_act, full_gateup)
    d_mixed = upstream.astype(F32) + rms_back(mixed, gain_two, d_normed_two)
    d_branch = d_mixed.astype(BF16)
    grad_out = rolled(dot_nn(context_t, d_branch), 0, (groups - group) % groups * group_width)
    d_context_t = dot_nt(out_rel, d_branch).astype(BF16)

    def scattered(grad):
        return lax.psum_scatter(grad.astype(BF16), ALL, scatter_dimension=0, tiled=True).astype(F32)

    shard_down = scattered(grad_down)
    shard_gateup = scattered(grad_gateup)
    shard_out = scattered(grad_out)

    head_size = LANES // 2
    d_queries, d_kvs, d_tables = [], [], []
    for head in range(group_heads):
        pieces = []
        for s in range(groups):
            piece = d_context_t[(s * group_heads + head) * head_size :][:head_size]
            pieces.append((s, piece))
        slots = [None] * groups
        for s, piece in pieces:
            slots[s] = from_group(piece, groups - s) if s else piece
        outs = attend_back(
            head,
            tok_rows,
            groups,
            splits,
            ints,
            buckets,
            query,
            jnp.concatenate(slots, axis=1),
            stats[head],
            probs[head],
            kvs,
        )
        d_queries.append(outs[0])
        d_kv = outs[1].astype(F32)
        for other in range(1, splits):
            d_kv = d_kv + from_split(outs[1 + other], splits - other).astype(F32)
        d_kvs.append(d_kv.astype(BF16))
        d_tables.append(jnp.sum(outs[-1], axis=1))

    d_query_t = jnp.concatenate(
        [
            from_group(slot_of(d_queries[head], s, 1), s) if s else slot_of(d_queries[head], 0, 1)
            for s in range(groups)
            for head in range(group_heads)
        ],
        axis=0,
    )
    d_kv_rows = jnp.concatenate(
        [
            from_group(slot_of(d_kvs[head], s, 0), s) if s else slot_of(d_kvs[head], 0, 0)
            for s in range(groups)
            for head in range(group_heads)
        ],
        axis=1,
    )
    d_normed = dot_tt(d_query_t, w_query) + dot_nt(d_kv_rows, w_kv)
    d_inputs = (d_mixed + rms_back(inputs, gain_one, d_normed)).astype(BF16)

    grad_group = jnp.concatenate(
        [dot_tt(normed, d) for d in d_queries] + [dot_tn(normed, d) for d in d_kvs], axis=1
    )
    shard_rows = width // (rows_apart * ring)
    grad_group = grad_group.reshape(rows_apart, groups, splits, shard_rows, 3 * group_width)
    held = lax.dynamic_index_in_dim(grad_group, split, 2, keepdims=False)
    for other in range(1, splits):
        target = (split + splits - other) % splits
        held = held + from_split(
            lax.dynamic_index_in_dim(grad_group, target, 2, keepdims=False), other
        )
    total = lax.dynamic_index_in_dim(held, batch, 0, keepdims=False)
    for step in range(1, rows_apart):
        total = total + lax.ppermute(
            lax.dynamic_index_in_dim(held, batch ^ step, 0, keepdims=False),
            "batch",
            [(i, i ^ step) for i in range(rows_apart)],
        )
    squares_group = jnp.sum(total * total, axis=(0, 1))
    columns = [lax.dynamic_index_in_dim(total, group, 0, keepdims=False)]
    for s in range(1, groups):
        columns.append(
            from_group(
                lax.dynamic_index_in_dim(total, (group + groups - s) % groups, 0, keepdims=False), s
            )
        )

    def unrolled(rel):
        absolute = rolled(rel, rel.ndim - 2, (groups - group) % groups)
        lead = absolute.shape[:-2]
        query_part = absolute[..., :group_width].reshape(*lead, 1, width)
        kv_part = absolute[..., group_width:].reshape(*lead, groups * group_heads, 2, head_size)
        kv_part = jnp.moveaxis(kv_part, -2, -3).reshape(*lead, 2, width)
        return jnp.concatenate([query_part, kv_part], axis=-2).reshape(*lead, 3 * width)

    shard_qkv = unrolled(jnp.stack(columns, axis=1))
    own_slot = (jnp.arange(groups) == 0).astype(F32)[:, None]
    squares_qkv = unrolled(own_slot * squares_group[None, :])
    table_local = jnp.stack(d_tables, axis=0)
    table_sum = lax.dynamic_update_slice_in_dim(
        jnp.zeros((heads, buckets), F32), table_local, group * group_heads, 0
    )
    table_total, column_qkv, column_out, column_gateup, column_down = lax.psum(
        (
            table_sum,
            squares_qkv,
            jnp.sum(shard_out * shard_out, axis=0),
            jnp.sum(shard_gateup * shard_gateup, axis=0),
            jnp.sum(shard_down * shard_down, axis=0),
        ),
        ALL,
    )
    shard_gain_one = jnp.sum(w_qkv.astype(F32) * shard_qkv, axis=1) / norm_one.astype(F32)
    shard_gain_two = jnp.sum(w_gateup.astype(F32) * shard_gateup, axis=1) / norm_two.astype(F32)
    new_row_qkv, new_col_qkv = factored(shard_qkv, column_qkv, row_qkv, col_qkv, width)
    new_row_out, new_col_out = factored(shard_out, column_out, row_out, col_out, width)
    new_row_gateup, new_col_gateup = factored(
        shard_gateup, column_gateup, row_gateup, col_gateup, width
    )
    new_row_down, new_col_down = factored(
        shard_down, column_down, row_down, col_down, full_down.shape[0]
    )
    return (
        result[None],
        d_inputs[None],
        shard_gain_one,
        shard_qkv,
        table_total.T,
        shard_out,
        shard_gain_two,
        shard_gateup,
        shard_down,
        new_row_qkv,
        new_col_qkv,
        new_row_out,
        new_col_out,
        new_row_gateup,
        new_col_gateup,
        new_row_down,
        new_col_down,
    )


def solution(mesh):
    split_rows = P(ALL, None)
    split_row = P(ALL)
    return jax.shard_map(
        shards,
        mesh=mesh,
        in_specs=(
            P("batch", "blk", None),
            P("batch", None),
            split_row,
            split_rows,
            P(),
            split_rows,
            split_row,
            split_rows,
            split_rows,
            P("batch", "blk", None),
            split_row,
            P(),
            split_row,
            P(),
            split_row,
            P(),
            split_row,
            P(),
        ),
        out_specs=(
            P("batch", "blk", None),
            P("batch", "blk", None),
            split_row,
            split_rows,
            P(),
            split_rows,
            split_row,
            split_rows,
            split_rows,
            split_row,
            P(),
            split_row,
            P(),
            split_row,
            P(),
            split_row,
            P(),
        ),
        check_vma=False,
    )
```

time: 1930 us -> 694 us (0.36)
  matrix products: 872 us -> 67.7 us
  other arithmetic: 290 us -> 48.9 us
  local copies, waits for them, and re-layouts: 221 us -> 45.9 us
  waiting for transfers between devices: 388 us -> 227 us
  Pallas kernels: 0 us -> 141 us
  starting transfers between devices: 19.3 us -> 94.7 us
  blocking collectives: 83.5 us -> 41.3 us
  loops' own time: 30.6 us -> 0 us
    dot_general x76 -> x19, matrix products: 872 us -> 67.7 us  [the longest x5 23.7 us: dot_nn(): return jnp.dot(left, right, preferred_element_type=F32)]
    reduce_scatter x4 -> x3, waiting for transfers between devices: 234 us -> 70.5 us  [scattered(): lax.psum_scatter(grad.astype(BF16), ALL, scatter_dimension=0, tiled=True)]
    pallas_call x0 -> x6, Pallas kernels: none -> 141 us  [the longest x3 78.9 us: attend_back(): pl.pallas_call(functools.partial(backward_kernel, tokens, groups, splits)...]
    or x16 -> x0, other arithmetic: 129 us -> none  [pair_layout(): (query_seg[:, None] == key_seg[None, :]) & ~key_pad[None, :]]
    convert_element_type x8 -> x0, local copies, waits for them, and re-layouts: 116 us -> none  [pair_grads(): dscores = (weights * (dprob - delta[:, :, None])).astype(jnp.bfloat16)]
    ppermute x30 -> x53, waiting for transfers between devices: 9.09 us -> 116 us  [the longest x6 55.2 us: line(): lax.ppermute(array, 'blk', [(i, i + step) for i in range(ring) if 0 <= i...]
    all_gather x6 -> x4, waiting for transfers between devices: 142 us -> 38.8 us  [the longest x1 38.8 us: shards(): full_down = lax.all_gather(w_down, ALL, axis=0, tiled=True)]
    unnamed x2 -> x0, blocking collectives: 83.5 us -> none
  transfers between devices with their start and end apart: 40 -> 60, of which waited for: 7 -> 26; matrix products, arithmetic and copies ran while one was open for 70% -> 18% of each run, Pallas kernels for 0% -> 21%
where the time goes in v1:
time: 694 us; the launch traced here: 685 us
  waiting for transfers between devices  227 us (33%)
  Pallas kernels  141 us (20%)
  starting transfers between devices  94.7 us (14%)
  matrix products  67.7 us (10%)
  other arithmetic  48.9 us (7%)
  local copies, waits for them, and re-layouts  45.9 us (7%)
  blocking collectives  41.3 us (6%)
  between operations  18.5 us (3%)
    pallas_call x3, Pallas kernels, attend_back(): pl.pallas_call(functools.partial(backward_kernel, tokens, groups, splits)...  78.9 us
    reduce_scatter x3, waiting for transfers between devices, scattered(): lax.psum_scatter(grad.astype(BF16), ALL, scatter_dimension=0, tiled=True)  70.5 us
    ppermute x39, starting transfers between devices, from_group(): lax.ppermute(array, 'blk', [(i, (i - step) % ring) for i in range(ring)])  69 us
    pallas_call x3, Pallas kernels, attend(): pl.pallas_call(functools.partial(forward_kernel, tokens, groups, splits),...  62.4 us
    ppermute x6, waiting for transfers between devices, line(): lax.ppermute(array, 'blk', [(i, i + step) for i in range(ring) if 0 <= i...  55.2 us
    ppermute x39, waiting for transfers between devices, from_group(): lax.ppermute(array, 'blk', [(i, (i - step) % ring) for i in range(ring)])  54.4 us
    psum x1, blocking collectives, shards(): lax.psum((table_sum, squares_qkv, jnp.sum(shard_out * shard_out, axis=0),...  41.3 us
    all_gather x1, waiting for transfers between devices, shards(): full_down = lax.all_gather(w_down, ALL, axis=0, tiled=True)  38.8 us
  transfers between devices with their start and end apart: 60, of which 26 were waited for; matrix products, arithmetic and copies ran while one was open for 18% of the time, Pallas kernels for 21%

profile of v1, /device:TPU:0, one launch (start us, length us, event | category | flops | bytes accessed | tf_op | source)
XLA Modules:
  0.0 685.5 jit_solution(1656680733861477965)
XLA Ops:
  12.4 5.6 collective-permute-start
  18.1 18.3 %collective-permute-done.1 = bf16[512,768]{1,0:T(8,128)(2,1)S(1)} collective-permute-done((bf16[512,768]{1,0:T(8,128)(2,1)}, bf16[512,768]{1,0:T(8,128)(2,1)S(1)}, u32[]{:S(2)}, u32[]{:S(2)}) %collective-permute-start.1) | collective-permute-done | bytes 786464 | tf_op jit(solution)/shard_map/ppermute | solution.py:449
  37.6 5.5 collective-permute-start.4
  43.1 20.5 %collective-permute-done.2 = bf16[512,768]{1,0:T(8,128)(2,1)S(1)} collective-permute-done((bf16[512,768]{1,0:T(8,128)(2,1)S(1)}, bf16[512,768]{1,0:T(8,128)(2,1)S(1)}, u32[]{:S(2)}, u32[]{:S(2)}) %collective-permute-start.2) | collective-permute-done | bytes 786464 | tf_op jit(solution)/shard_map/ppermute | solution.py:449
  66.2 6.2 collective-permute-start.5
  73.8 15.1 %collective-permute-done.3 = bf16[512,768]{1,0:T(8,128)(2,1)} collective-permute-done((bf16[512,768]{1,0:T(8,128)(2,1)S(1)}, bf16[512,768]{1,0:T(8,128)(2,1)}, u32[]{:S(2)}, u32[]{:S(2)}) %collective-permute-start.3) | collective-permute-done | bytes 786464 | tf_op jit(solution)/shard_map/ppermute | solution.py:449
  92.9 4.0 slice.277
  96.9 5.7 copy.58
  102.6 3.3 fusion.9
  107.9 2.1 convert_reduce_fusion
  110.6 6.9 %fusion.2 = bf16[2048,768]{1,0:T(8,128)(2,1)S(1)} fusion(f32[768]{0:T(1024)S(1)} %get-tuple-element.60, f32[2048]{0:T(1024)S(1)} %add_rsqrt_fusion, bf16[512,768]{1,0:T(8,128)(2,1)S(1)} %copy-done.18, bf16[512,768]{1,0:T(8,128)(2,1)S(1)} %copy-done.14, bf16[512,768]{1,0:T(8,128)(2,1)S(1)} %copy-done.16, bf16[512,768]{1,0:T(8,128)(2,1)S(1)} %bitcast.104), kind=kLoop, calls=%fused_computation.7 | loop fusion | flops 17301504 | bytes 6302720 | tf_op jit(solution)/shard_map/convert_element_type | solution.py:490
  117.5 3.0 convolution_convert_fusion.2.refs_0_
  123.1 3.0 convolution_convert_fusion.3.query
  126.1 20.8 %attend.3 = (bf16[16384,512]{1,0:T(8,128)(2,1)}, bf16[64,2048]{1,0:T(8,128)(2,1)}, f32[80,2048]{1,0:T(8,128)}) custom-call(s32[5]{0:T(128)} %pad_add_fusion.ints, f32[1,32]{1,0:T(1,128)} %get-tuple-element.144.table, bf16[2048,384]{1,0:T(8,128)(2,1)} %convolution_convert_fusion.3.query, bf16[2048,384]{1,0:T(8,128)(2,1)} %convolution_convert_fusion.2.refs_0_, ...), custom_call_target="tpu_custom_call" | custom-call | flops 8589934592 | bytes 16777216 | tf_op jit(solution)/shard_map/attend/pallas_call | solution.py:326
  149.9 2.1 collective-permute-start.10
  153.8 20.8 %attend.4 = (bf16[16384,512]{1,0:T(8,128)(2,1)}, bf16[64,2048]{1,0:T(8,128)(2,1)}, f32[80,2048]{1,0:T(8,128)}) custom-call(s32[5]{0:T(128)} %pad_add_fusion.ints, f32[1,32]{1,0:T(1,128)} %get-tuple-element.143.table, bf16[2048,384]{1,0:T(8,128)(2,1)} %convolution_convert_fusion.3.query, bf16[2048,384]{1,0:T(8,128)(2,1)} %convolution_convert_fusion.2.refs_0_, ...), custom_call_target="tpu_custom_call" | custom-call | flops 8589934592 | bytes 16777216 | tf_op jit(solution)/shard_map/attend/pallas_call | solution.py:326
  177.4 20.8 %attend.5 = (bf16[16384,512]{1,0:T(8,128)(2,1)}, bf16[64,2048]{1,0:T(8,128)(2,1)}, f32[80,2048]{1,0:T(8,128)}) custom-call(s32[5]{0:T(128)} %pad_add_fusion.ints, f32[1,32]{1,0:T(1,128)} %get-tuple-element.142.table, bf16[2048,384]{1,0:T(8,128)(2,1)} %convolution_convert_fusion.3.query, bf16[2048,384]{1,0:T(8,128)(2,1)} %convolution_convert_fusion.2.refs_0_, ...), custom_call_target="tpu_custom_call" | custom-call | flops 8589934592 | bytes 16777216 | tf_op jit(solution)/shard_map/attend/pallas_call | solution.py:326
  199.8 2.8 collective-permute-start.8
  203.2 3.3 collective-permute-done.8
  206.5 3.3 collective-permute-start.9
  212.2 2.2 collective-permute-start.15
  215.1 2.0 collective-permute-start.12
  218.3 2.1 collective-permute-done.12
  223.0 3.9 multiply_reduce_fusion.1
  226.9 10.1 %fusion.38 = f32[512,4096]{1,0:T(8,128)} fusion(bf16[768,4096]{1,0:T(8,128)(2,1)} %all-gather.9.cloned.1.call-done, f32[512,768]{1,0:T(8,128)} %get-tuple-element.146, f32[768]{0:T(1024)S(1)} %get-tuple-element.59, f32[512]{0:T(512)S(1)} %get-tuple-element.141), kind=kOutput, calls=%fused_computation.173 | convolution fusion | flops 3222405120 | bytes 16258048 | tf_op jit(solution)/shard_map/dot_general | solution.py:53
  237.0 38.8 %all-gather.11.cloned.1.call-done = bf16[2048,768]{1,0:T(8,128)(2,1)} async-done(((bf16[64,768]{1,0:T(8,128)(2,1)}), bf16[2048,768]{1,0:T(8,128)(2,1)}) %all-gather.11.cloned.1.call-update) | async-done | bytes 3145744 | tf_op jit(solution)/shard_map/all_gather | solution.py:474
  275.8 10.6 %fusion.6 = (bf16[512,2048]{1,0:T(8,128)(2,1)S(1)}, bf16[512,2048]{1,0:T(8,128)(2,1)S(1)}, bf16[512,2048]{1,0:T(8,128)(2,1)}) fusion(f32[512,4096]{1,0:T(8,128)} %fusion.38, bf16[2048,768]{1,0:T(8,128)(2,1)} %all-gather.11.cloned.1.call-done, bf16[1,512,768]{2,1,0:T(8,128)(2,1)} %param.27), kind=kOutput, calls=%fused_computation.17 | convolution fusion | flops 1642070016 | bytes 18612224 | tf_op jit(solution)/shard_map/dot_general | solution.py:61
  286.4 3.6 multiply_reduce_fusion
  293.5 2.7 fusion.12
  296.2 5.3 convolution_convert_fusion.1
  302.2 2.4 slice.296
  304.6 2.3 convolution_convert_fusion.4
  307.7 2.1 collective-permute-start.24
  309.8 2.3 collective-permute-start.18
  312.7 2.0 collective-permute-start.16
  314.8 5.9 convolution_convert_fusion
  320.6 5.7 fusion.20
  327.2 3.0 collective-permute-start.21
  331.8 26.2 %attend_back.3 = (bf16[64,2048]{1,0:T(8,128)(2,1)}, bf16[2048,128]{1,0:T(8,128)(2,1)}, bf16[2048,128]{1,0:T(8,128)(2,1)}, f32[32,128]{1,0:T(8,128)}) custom-call(s32[5]{0:T(128)} %pad_add_fusion.ints, bf16[2048,384]{1,0:T(8,128)(2,1)} %convolution_convert_fusion.3.query, bf16[64,2048]{1,0:T(8,128)(2,1)} %pad_maximum_fusion.6.d_context, ...), custom_call_target="tpu_custom_call" | custom-call | flops 17179869184 | bytes 16777216 | tf_op jit(solution)/shard_map/attend_back/pallas_call | solution.py:362
  358.1 2.3 convolution_dynamic-update-slice_fusion.5
  362.6 26.4 %attend_back.5 = (bf16[64,2048]{1,0:T(8,128)(2,1)}, bf16[2048,128]{1,0:T(8,128)(2,1)}, bf16[2048,128]{1,0:T(8,128)(2,1)}, f32[32,128]{1,0:T(8,128)}) custom-call(s32[5]{0:T(128)} %pad_add_fusion.ints, bf16[2048,384]{1,0:T(8,128)(2,1)} %convolution_convert_fusion.3.query, bf16[64,2048]{1,0:T(8,128)(2,1)} %pad_maximum_fusion.8.d_context, ...), custom_call_target="tpu_custom_call" | custom-call | flops 17179869184 | bytes 16777216 | tf_op jit(solution)/shard_map/attend_back/pallas_call | solution.py:362
  392.2 26.3 %attend_back.4 = (bf16[64,2048]{1,0:T(8,128)(2,1)}, bf16[2048,128]{1,0:T(8,128)(2,1)}, bf16[2048,128]{1,0:T(8,128)(2,1)}, f32[32,128]{1,0:T(8,128)}) custom-call(s32[5]{0:T(128)} %pad_add_fusion.ints, bf16[2048,384]{1,0:T(8,128)(2,1)} %convolution_convert_fusion.3.query, bf16[64,2048]{1,0:T(8,128)(2,1)} %pad_maximum_fusion.7.d_context, ...), custom_call_target="tpu_custom_call" | custom-call | flops 17179869184 | bytes 16777216 | tf_op jit(solution)/shard_map/attend_back/pallas_call | solution.py:362
  420.5 2.8 collective-permute-start.31
  425.9 2.3 convolution_dynamic-update-slice_fusion.4
  432.5 2.4 collective-permute-done.26
  435.0 3.2 collective-permute-start.27
  438.8 2.1 collective-permute-done.27
  441.8 4.6 collective-permute-done.28
  447.2 5.0 collective-permute-done.29
  452.8 8.1 %collective-permute-done.30 = bf16[64,512]{1,0:T(8,128)(2,1)S(1)} collective-permute-done((bf16[64,512]{1,0:T(8,128)(2,1)}, bf16[64,512]{1,0:T(8,128)(2,1)S(1)}, u32[]{:S(2)}, u32[]{:S(2)}) %collective-permute-start.30) | collective-permute-done | bytes 65568 | tf_op jit(solution)/shard_map/ppermute | solution.py:455
  460.9 4.9 collective-permute-start.32
  467.1 3.9 collective-permute-done.32
  482.8 2.1 copy.54
  488.1 2.2 collective-permute-start.37
  491.1 8.8 %collective-permute-done.37 = bf16[512,128]{1,0:T(8,128)(2,1)S(1)} collective-permute-done((bf16[512,128]{1,0:T(8,128)(2,1)S(1)}, bf16[512,128]{1,0:T(8,128)(2,1)S(1)}, u32[]{:S(2)}, u32[]{:S(2)}) %collective-permute-start.37) | collective-permute-done | bytes 131104 | tf_op jit(solution)/shard_map/ppermute | solution.py:455
  502.2 3.9 collective-permute-start.44
  506.2 8.0 %collective-permute-start.41 = (bf16[512,128]{1,0:T(8,128)(2,1)S(1)}, bf16[512,128]{1,0:T(8,128)(2,1)S(1)}, u32[]{:S(2)}, u32[]{:S(2)}) collective-permute-start(bf16[512,128]{1,0:T(8,128)(2,1)S(1)} %get-tuple-element.103), channel_id=1, source_target_pairs={{0,4},{1,5},{2,6},{3,7},{4,0},{5,1},{6,2},{7,3},{8,12},{9,13},{10,... | collective-permute-start | bytes 393224 | tf_op jit(solution)/shard_map/ppermute | solution.py:455
  514.4 3.5 collective-permute-done.41
  517.9 4.7 collective-permute-start.45
  522.6 3.2 collective-permute-done.42
  537.8 3.7 collective-permute-done.49
  545.5 2.4 collective-permute-start.50
  555.6 70.5 %reduce-scatter.6.cloned.1.call-done = bf16[24,4096]{1,0:T(8,128)(2,1)} async-done(((bf16[768,4096]{1,0:T(8,128)(2,1)}), bf16[24,4096]{1,0:T(8,128)(2,1)}) %reduce-scatter.6.cloned.1.call-update) | async-done | bytes 196624 | tf_op jit(solution)/shard_map/reduce_scatter | solution.py:542
  628.5 41.3 %all-reduce.2 = (f32[32,12]{0,1:T(8,128)}, f32[2304]{0:T(1024)S(1)}, f32[768]{0:T(1024)S(1)}, f32[4096]{0:T(1024)S(1)}, f32[768]{0:T(1024)S(1)}) all-reduce(f32[32,12]{0,1:T(8,128)S(1)} %bitcast.114, f32[2304]{0:T(1024)S(1)} %reshape.179, f32[768]{0:T(1024)S(1)} %get-tuple-element.68, ...), channel_id=1, replica_groups=mesh['batch'=4,'blk'=8] {'batch','blk'}, use_global_device_ids=true, to_apply=%region_10.11 | all-reduce | flops 8320 | bytes 66560 | tf_op jit(solution)/shard_map/psum | solution.py:639
  (333 shorter events, 112.4 us)
Async XLA Ops:
  7.2 85.6 %all-gather.5.cloned.1.call-start = ((), (), s32[]{:S(2)}) async-start(), calls=%async_computation.3 | async-start | bytes 3852288 | tf_op jit(solution)/shard_map/all_gather | solution.py:471
  9.6 213.4 %all-gather.7.cloned.1.call-start = ((), (), s32[]{:S(2)}) async-start(), calls=%async_computation.4 | async-start | bytes 1216512 | tf_op jit(solution)/shard_map/all_gather | solution.py:472
  10.4 216.6 %all-gather.9.cloned.1.call-start = ((), (), s32[]{:S(2)}) async-start(), calls=%async_computation.5 | async-start | bytes 6488064 | tf_op jit(solution)/shard_map/all_gather | solution.py:473
  11.1 264.7 %all-gather.11.cloned.1.call-start = ((), (), s32[]{:S(2)}) async-start(), calls=%async_computation.6 | async-start | bytes 3244032 | tf_op jit(solution)/shard_map/all_gather | solution.py:474
  11.1 25.2 %collective-permute-start.1 = (bf16[512,768]{1,0:T(8,128)(2,1)}, bf16[512,768]{1,0:T(8,128)(2,1)S(1)}, u32[]{:S(2)}, u32[]{:S(2)}) collective-permute-start(bf16[512,768]{1,0:T(8,128)(2,1)} %bitcast.101), channel_id=1, source_target_pairs={{2,0},{3,1},{4,2},{5,3},{6,4},{7,5},{10,8},{11,9},{12,10},{13,11},... | collective-permute-start | bytes 2359304 | tf_op jit(solution)/shard_map/ppermute | solution.py:449
  12.4 25.2 %collective-permute-start = (bf16[512,768]{1,0:T(8,128)(2,1)}, bf16[512,768]{1,0:T(8,128)(2,1)S(1)}, u32[]{:S(2)}, u32[]{:S(2)}) collective-permute-start(bf16[512,768]{1,0:T(8,128)(2,1)} %bitcast.102), channel_id=1, source_target_pairs={{0,2},{1,3},{2,4},{3,5},{4,6},{5,7},{8,10},{9,11},{10,12},{11,13},... | collective-permute-start | bytes 2359304 | tf_op jit(solution)/shard_map/ppermute | solution.py:449
  36.3 27.3 %collective-permute-start.2 = (bf16[512,768]{1,0:T(8,128)(2,1)S(1)}, bf16[512,768]{1,0:T(8,128)(2,1)S(1)}, u32[]{:S(2)}, u32[]{:S(2)}) collective-permute-start(bf16[512,768]{1,0:T(8,128)(2,1)S(1)} %collective-permute-done.1), channel_id=1, source_target_pairs={{2,0},{3,1},{4,2},{5,3},{6,4},{7,5},{10,8},{11,9},{12,10},{13,11},... | collective-permute-start | bytes 2359304 | tf_op jit(solution)/shard_map/ppermute | solution.py:449
  37.6 28.6 %collective-permute-start.4 = (bf16[512,768]{1,0:T(8,128)(2,1)S(1)}, bf16[512,768]{1,0:T(8,128)(2,1)}, u32[]{:S(2)}, u32[]{:S(2)}) collective-permute-start(bf16[512,768]{1,0:T(8,128)(2,1)S(1)} %collective-permute-done), channel_id=1, source_target_pairs={{0,2},{1,3},{2,4},{3,5},{4,6},{5,7},{8,10},{9,11},{10,12},{11,13},... | collective-permute-start | bytes 2359304 | tf_op jit(solution)/shard_map/ppermute | solution.py:449
  63.6 25.3 %collective-permute-start.3 = (bf16[512,768]{1,0:T(8,128)(2,1)S(1)}, bf16[512,768]{1,0:T(8,128)(2,1)}, u32[]{:S(2)}, u32[]{:S(2)}) collective-permute-start(bf16[512,768]{1,0:T(8,128)(2,1)S(1)} %collective-permute-done.2), channel_id=1, source_target_pairs={{2,0},{3,1},{4,2},{5,3},{6,4},{7,5},{10,8},{11,9},{12,10},{13,11},... | collective-permute-start | bytes 2359304 | tf_op jit(solution)/shard_map/ppermute | solution.py:449
  66.2 24.1 %collective-permute-start.5 = (bf16[512,768]{1,0:T(8,128)(2,1)}, bf16[512,768]{1,0:T(8,128)(2,1)}, u32[]{:S(2)}, u32[]{:S(2)}) collective-permute-start(bf16[512,768]{1,0:T(8,128)(2,1)} %collective-permute-done.4), channel_id=1, source_target_pairs={{0,2},{1,3},{2,4},{3,5},{4,6},{5,7},{8,10},{9,11},{10,12},{11,13},... | collective-permute-start | bytes 2359304 | tf_op jit(solution)/shard_map/ppermute | solution.py:449
  120.5 5.6 collective-permute-start.6
  120.5 414.4 %reduce-scatter.4.cloned.1.call-start = ((), (), s32[]{:S(2)}) async-start(), calls=%async_computation.7 | async-start | bytes 1216512 | tf_op jit(solution)/shard_map/reduce_scatter | solution.py:542
  148.5 72.6 %collective-permute-start.13 = (bf16[64,512]{1,0:T(8,128)(2,1)S(1)}, bf16[64,512]{1,0:T(8,128)(2,1)S(1)}, u32[]{:S(2)}, u32[]{:S(2)}) collective-permute-start(bf16[64,512]{1,0:T(8,128)(2,1)S(1)} %get-tuple-element.130), channel_id=1, source_target_pairs={{0,2},{1,3},{2,4},{3,5},{4,6},{5,7},{6,0},{7,1},{8,10},{9,11},{10,... | collective-permute-start | bytes 196616 | tf_op jit(solution)/shard_map/ppermute | solution.py:455
  149.9 65.1 %collective-permute-start.10 = (bf16[64,512]{1,0:T(8,128)(2,1)S(1)}, bf16[64,512]{1,0:T(8,128)(2,1)S(1)}, u32[]{:S(2)}, u32[]{:S(2)}) collective-permute-start(bf16[64,512]{1,0:T(8,128)(2,1)S(1)} %get-tuple-element.131), channel_id=1, source_target_pairs={{0,4},{1,5},{2,6},{3,7},{4,0},{5,1},{6,2},{7,3},{8,12},{9,13},{10,... | collective-permute-start | bytes 196616 | tf_op jit(solution)/shard_map/ppermute | solution.py:455
  152.1 47.7 %collective-permute-start.7 = (bf16[64,512]{1,0:T(8,128)(2,1)S(1)}, bf16[64,512]{1,0:T(8,128)(2,1)S(1)}, u32[]{:S(2)}, u32[]{:S(2)}) collective-permute-start(bf16[64,512]{1,0:T(8,128)(2,1)S(1)} %get-tuple-element.132), channel_id=1, source_target_pairs={{0,6},{1,7},{2,0},{3,1},{4,2},{5,3},{6,4},{7,5},{8,14},{9,15},{10,... | collective-permute-start | bytes 196616 | tf_op jit(solution)/shard_map/ppermute | solution.py:455
  176.2 45.6 %collective-permute-start.14 = (bf16[64,512]{1,0:T(8,128)(2,1)S(1)}, bf16[64,512]{1,0:T(8,128)(2,1)S(1)}, u32[]{:S(2)}, u32[]{:S(2)}) collective-permute-start(bf16[64,512]{1,0:T(8,128)(2,1)S(1)} %get-tuple-element.126), channel_id=1, source_target_pairs={{0,2},{1,3},{2,4},{3,5},{4,6},{5,7},{6,0},{7,1},{8,10},{9,11},{10,... | collective-permute-start | bytes 196616 | tf_op jit(solution)/shard_map/ppermute | solution.py:455
  176.7 41.1 %collective-permute-start.11 = (bf16[64,512]{1,0:T(8,128)(2,1)S(1)}, bf16[64,512]{1,0:T(8,128)(2,1)S(1)}, u32[]{:S(2)}, u32[]{:S(2)}) collective-permute-start(bf16[64,512]{1,0:T(8,128)(2,1)S(1)} %get-tuple-element.127), channel_id=1, source_target_pairs={{0,4},{1,5},{2,6},{3,7},{4,0},{5,1},{6,2},{7,3},{8,12},{9,13},{10,... | collective-permute-start | bytes 196616 | tf_op jit(solution)/shard_map/ppermute | solution.py:455
  199.8 6.7 collective-permute-start.8
  206.5 5.7 collective-permute-start.9
  212.2 10.2 %collective-permute-start.15 = (bf16[64,512]{1,0:T(8,128)(2,1)S(1)}, bf16[64,512]{1,0:T(8,128)(2,1)S(1)}, u32[]{:S(2)}, u32[]{:S(2)}) collective-permute-start(bf16[64,512]{1,0:T(8,128)(2,1)S(1)} %get-tuple-element.122), channel_id=1, source_target_pairs={{0,2},{1,3},{2,4},{3,5},{4,6},{5,7},{6,0},{7,1},{8,10},{9,11},{10,... | collective-permute-start | bytes 196616 | tf_op jit(solution)/shard_map/ppermute | solution.py:455
  215.1 5.4 collective-permute-start.12
  296.2 257.7 %reduce-scatter.8.cloned.1.call-start = ((), (), s32[]{:S(2)}) async-start(), calls=%async_computation.9 | async-start | bytes 3244032 | tf_op jit(solution)/shard_map/reduce_scatter | solution.py:542
  301.5 324.6 %reduce-scatter.6.cloned.1.call-start = ((), (), s32[]{:S(2)}) async-start(), calls=%async_computation.8 | async-start | bytes 6488064 | tf_op jit(solution)/shard_map/reduce_scatter | solution.py:542
  307.7 52.7 %collective-permute-start.24 = (bf16[64,512]{1,0:T(8,128)(2,1)}, bf16[64,512]{1,0:T(8,128)(2,1)}, u32[]{:S(2)}, u32[]{:S(2)}) collective-permute-start(bf16[64,512]{1,0:T(8,128)(2,1)} %get-tuple-element.87), channel_id=1, source_target_pairs={{0,6},{1,7},{2,0},{3,1},{4,2},{5,3},{6,4},{7,5},{8,14},{9,15},{10,... | collective-permute-start | bytes 196616 | tf_op jit(solution)/shard_map/ppermute | solution.py:455
  309.8 51.2 %collective-permute-start.23 = (bf16[64,512]{1,0:T(8,128)(2,1)}, bf16[64,512]{1,0:T(8,128)(2,1)}, u32[]{:S(2)}, u32[]{:S(2)}) collective-permute-start(bf16[64,512]{1,0:T(8,128)(2,1)} %get-tuple-element.88), channel_id=1, source_target_pairs={{0,4},{1,5},{2,6},{3,7},{4,0},{5,1},{6,2},{7,3},{8,12},{9,13},{10,... | collective-permute-start | bytes 196616 | tf_op jit(solution)/shard_map/ppermute | solution.py:455
  309.8 16.6 %collective-permute-start.18 = (bf16[64,512]{1,0:T(8,128)(2,1)}, bf16[64,512]{1,0:T(8,128)(2,1)}, u32[]{:S(2)}, u32[]{:S(2)}) collective-permute-start(bf16[64,512]{1,0:T(8,128)(2,1)} %get-tuple-element.94), channel_id=1, source_target_pairs={{0,6},{1,7},{2,0},{3,1},{4,2},{5,3},{6,4},{7,5},{8,14},{9,15},{10,... | collective-permute-start | bytes 196616 | tf_op jit(solution)/shard_map/ppermute | solution.py:455
  312.1 15.1 %collective-permute-start.17 = (bf16[64,512]{1,0:T(8,128)(2,1)}, bf16[64,512]{1,0:T(8,128)(2,1)}, u32[]{:S(2)}, u32[]{:S(2)}) collective-permute-start(bf16[64,512]{1,0:T(8,128)(2,1)} %get-tuple-element.95), channel_id=1, source_target_pairs={{0,4},{1,5},{2,6},{3,7},{4,0},{5,1},{6,2},{7,3},{8,12},{9,13},{10,... | collective-permute-start | bytes 196616 | tf_op jit(solution)/shard_map/ppermute | solution.py:455
  312.7 17.5 %collective-permute-start.16 = (bf16[64,512]{1,0:T(8,128)(2,1)}, bf16[64,512]{1,0:T(8,128)(2,1)}, u32[]{:S(2)}, u32[]{:S(2)}) collective-permute-start(bf16[64,512]{1,0:T(8,128)(2,1)} %get-tuple-element.96), channel_id=1, source_target_pairs={{0,2},{1,3},{2,4},{3,5},{4,6},{5,7},{6,0},{7,1},{8,10},{9,11},{10,... | collective-permute-start | bytes 196616 | tf_op jit(solution)/shard_map/ppermute | solution.py:455
  326.4 34.6 %collective-permute-start.22 = (bf16[64,512]{1,0:T(8,128)(2,1)S(1)}, bf16[64,512]{1,0:T(8,128)(2,1)S(1)}, u32[]{:S(2)}, u32[]{:S(2)}) collective-permute-start(bf16[64,512]{1,0:T(8,128)(2,1)S(1)} %copy-done.43), channel_id=1, source_target_pairs={{0,2},{1,3},{2,4},{3,5},{4,6},{5,7},{6,0},{7,1},{8,10},{9,11},{10,... | collective-permute-start | bytes 196616 | tf_op jit(solution)/shard_map/ppermute | solution.py:455
  327.2 63.4 %collective-permute-start.21 = (bf16[64,512]{1,0:T(8,128)(2,1)S(1)}, bf16[64,512]{1,0:T(8,128)(2,1)}, u32[]{:S(2)}, u32[]{:S(2)}) collective-permute-start(bf16[64,512]{1,0:T(8,128)(2,1)S(1)} %get-tuple-element.90), channel_id=1, source_target_pairs={{0,6},{1,7},{2,0},{3,1},{4,2},{5,3},{6,4},{7,5},{8,14},{9,15},{10,... | collective-permute-start | bytes 196616 | tf_op jit(solution)/shard_map/ppermute | solution.py:455
  330.2 60.4 %collective-permute-start.20 = (bf16[64,512]{1,0:T(8,128)(2,1)S(1)}, bf16[64,512]{1,0:T(8,128)(2,1)}, u32[]{:S(2)}, u32[]{:S(2)}) collective-permute-start(bf16[64,512]{1,0:T(8,128)(2,1)S(1)} %get-tuple-element.91), channel_id=1, source_target_pairs={{0,4},{1,5},{2,6},{3,7},{4,0},{5,1},{6,2},{7,3},{8,12},{9,13},{10,... | collective-permute-start | bytes 196616 | tf_op jit(solution)/shard_map/ppermute | solution.py:455
  360.4 30.2 %collective-permute-start.19 = (bf16[64,512]{1,0:T(8,128)(2,1)S(1)}, bf16[64,512]{1,0:T(8,128)(2,1)S(1)}, u32[]{:S(2)}, u32[]{:S(2)}) collective-permute-start(bf16[64,512]{1,0:T(8,128)(2,1)S(1)} %get-tuple-element.92), channel_id=1, source_target_pairs={{0,2},{1,3},{2,4},{3,5},{4,6},{5,7},{6,0},{7,1},{8,10},{9,11},{10,... | collective-permute-start | bytes 196616 | tf_op jit(solution)/shard_map/ppermute | solution.py:455
  420.0 53.7 %collective-permute-start.34 = (bf16[2048,128]{1,0:T(8,128)(2,1)}, bf16[2048,128]{1,0:T(8,128)(2,1)}, u32[]{:S(2)}, u32[]{:S(2)}) collective-permute-start(bf16[2048,128]{1,0:T(8,128)(2,1)} %get-tuple-element.51), channel_id=1, source_target_pairs={{1,0},{0,1},{3,2},{2,3},{5,4},{4,5},{7,6},{6,7},{9,8},{8,9},{11,10... | collective-permute-start | bytes 1572872 | tf_op jit(solution)/shard_map/ppermute | solution.py:462
  420.0 55.1 %collective-permute-start.35 = (bf16[2048,128]{1,0:T(8,128)(2,1)}, bf16[2048,128]{1,0:T(8,128)(2,1)}, u32[]{:S(2)}, u32[]{:S(2)}) collective-permute-start(bf16[2048,128]{1,0:T(8,128)(2,1)} %get-tuple-element.53), channel_id=1, source_target_pairs={{1,0},{0,1},{3,2},{2,3},{5,4},{4,5},{7,6},{6,7},{9,8},{8,9},{11,10... | collective-permute-start | bytes 1572872 | tf_op jit(solution)/shard_map/ppermute | solution.py:462
  420.5 58.8 %collective-permute-start.36 = (bf16[2048,128]{1,0:T(8,128)(2,1)}, bf16[2048,128]{1,0:T(8,128)(2,1)}, u32[]{:S(2)}, u32[]{:S(2)}) collective-permute-start(bf16[2048,128]{1,0:T(8,128)(2,1)} %get-tuple-element.55), channel_id=1, source_target_pairs={{1,0},{0,1},{3,2},{2,3},{5,4},{4,5},{7,6},{6,7},{9,8},{8,9},{11,10... | collective-permute-start | bytes 1572872 | tf_op jit(solution)/shard_map/ppermute | solution.py:462
  420.5 45.9 %collective-permute-start.31 = (bf16[64,512]{1,0:T(8,128)(2,1)}, bf16[64,512]{1,0:T(8,128)(2,1)S(1)}, u32[]{:S(2)}, u32[]{:S(2)}) collective-permute-start(bf16[64,512]{1,0:T(8,128)(2,1)} %get-tuple-element.118), channel_id=1, source_target_pairs={{0,2},{1,3},{2,4},{3,5},{4,6},{5,7},{6,0},{7,1},{8,10},{9,11},{10,... | collective-permute-start | bytes 196616 | tf_op jit(solution)/shard_map/ppermute | solution.py:455
  423.3 7.1 %collective-permute-start.25 = (bf16[64,512]{1,0:T(8,128)(2,1)}, bf16[64,512]{1,0:T(8,128)(2,1)S(1)}, u32[]{:S(2)}, u32[]{:S(2)}) collective-permute-start(bf16[64,512]{1,0:T(8,128)(2,1)} %get-tuple-element.120), channel_id=1, source_target_pairs={{0,6},{1,7},{2,0},{3,1},{4,2},{5,3},{6,4},{7,5},{8,14},{9,15},{10,... | collective-permute-start | bytes 196616 | tf_op jit(solution)/shard_map/ppermute | solution.py:455
  430.4 4.5 collective-permute-start.26
  435.0 6.0 collective-permute-start.27
  440.9 5.5 collective-permute-start.28
  446.4 5.7 collective-permute-start.29
  452.2 8.7 %collective-permute-start.30 = (bf16[64,512]{1,0:T(8,128)(2,1)}, bf16[64,512]{1,0:T(8,128)(2,1)S(1)}, u32[]{:S(2)}, u32[]{:S(2)}) collective-permute-start(bf16[64,512]{1,0:T(8,128)(2,1)} %get-tuple-element.111), channel_id=1, source_target_pairs={{0,4},{1,5},{2,6},{3,7},{4,0},{5,1},{6,2},{7,3},{8,12},{9,13},{10,... | collective-permute-start | bytes 196616 | tf_op jit(solution)/shard_map/ppermute | solution.py:455
  460.9 10.0 %collective-permute-start.32 = (bf16[64,512]{1,0:T(8,128)(2,1)}, bf16[64,512]{1,0:T(8,128)(2,1)S(1)}, u32[]{:S(2)}, u32[]{:S(2)}) collective-permute-start(bf16[64,512]{1,0:T(8,128)(2,1)} %get-tuple-element.114), channel_id=1, source_target_pairs={{0,2},{1,3},{2,4},{3,5},{4,6},{5,7},{6,0},{7,1},{8,10},{9,11},{10,... | collective-permute-start | bytes 196616 | tf_op jit(solution)/shard_map/ppermute | solution.py:455
  466.4 6.6 collective-permute-start.33
  485.0 45.6 %collective-permute-start.46 = (f32[4,4,24,576]{3,2,1,0:T(8,128)S(1)}, f32[4,4,24,576]{3,2,1,0:T(8,128)S(1)}, u32[]{:S(2)}, u32[]{:S(2)}) collective-permute-start(f32[4,4,24,576]{3,2,1,0:T(8,128)S(1)} %dynamic-slice_bitcast_fusion), channel_id=1, source_target_pairs={{1,0},{0,1},{3,2},{2,3},{5,4},{4,5},{7,6},{6,7},{9,8},{8,9},{11,10... | collective-permute-start | bytes 2654216 | tf_op jit(solution)/shard_map/ppermute | solution.py:462
  486.4 39.5 %collective-permute-start.43 = (bf16[512,128]{1,0:T(8,128)(2,1)S(1)}, bf16[512,128]{1,0:T(8,128)(2,1)S(1)}, u32[]{:S(2)}, u32[]{:S(2)}) collective-permute-start(bf16[512,128]{1,0:T(8,128)(2,1)S(1)} %get-tuple-element.106), channel_id=1, source_target_pairs={{0,2},{1,3},{2,4},{3,5},{4,6},{5,7},{6,0},{7,1},{8,10},{9,11},{10,... | collective-permute-start | bytes 393224 | tf_op jit(solution)/shard_map/ppermute | solution.py:455
  486.4 27.8 %collective-permute-start.40 = (bf16[512,128]{1,0:T(8,128)(2,1)S(1)}, bf16[512,128]{1,0:T(8,128)(2,1)S(1)}, u32[]{:S(2)}, u32[]{:S(2)}) collective-permute-start(bf16[512,128]{1,0:T(8,128)(2,1)S(1)} %get-tuple-element.107), channel_id=1, source_target_pairs={{0,4},{1,5},{2,6},{3,7},{4,0},{5,1},{6,2},{7,3},{8,12},{9,13},{10,... | collective-permute-start | bytes 393224 | tf_op jit(solution)/shard_map/ppermute | solution.py:455
  488.1 11.8 %collective-permute-start.37 = (bf16[512,128]{1,0:T(8,128)(2,1)S(1)}, bf16[512,128]{1,0:T(8,128)(2,1)S(1)}, u32[]{:S(2)}, u32[]{:S(2)}) collective-permute-start(bf16[512,128]{1,0:T(8,128)(2,1)S(1)} %get-tuple-element.108), channel_id=1, source_target_pairs={{0,6},{1,7},{2,0},{3,1},{4,2},{5,3},{6,4},{7,5},{8,14},{9,15},{10,... | collective-permute-start | bytes 393224 | tf_op jit(solution)/shard_map/ppermute | solution.py:455
  490.4 11.9 %collective-permute-start.38 = (bf16[512,128]{1,0:T(8,128)(2,1)S(1)}, bf16[512,128]{1,0:T(8,128)(2,1)S(1)}, u32[]{:S(2)}, u32[]{:S(2)}) collective-permute-start(bf16[512,128]{1,0:T(8,128)(2,1)S(1)} %get-tuple-element.104), channel_id=1, source_target_pairs={{0,6},{1,7},{2,0},{3,1},{4,2},{5,3},{6,4},{7,5},{8,14},{9,15},{10,... | collective-permute-start | bytes 393224 | tf_op jit(solution)/shard_map/ppermute | solution.py:455
  499.9 6.3 collective-permute-start.39
  502.2 23.7 %collective-permute-start.44 = (bf16[512,128]{1,0:T(8,128)(2,1)S(1)}, bf16[512,128]{1,0:T(8,128)(2,1)S(1)}, u32[]{:S(2)}, u32[]{:S(2)}) collective-permute-start(bf16[512,128]{1,0:T(8,128)(2,1)S(1)} %get-tuple-element.102), channel_id=1, source_target_pairs={{0,2},{1,3},{2,4},{3,5},{4,6},{5,7},{6,0},{7,1},{8,10},{9,11},{10,... | collective-permute-start | bytes 393224 | tf_op jit(solution)/shard_map/ppermute | solution.py:455
  506.2 11.7 %collective-permute-start.41 = (bf16[512,128]{1,0:T(8,128)(2,1)S(1)}, bf16[512,128]{1,0:T(8,128)(2,1)S(1)}, u32[]{:S(2)}, u32[]{:S(2)}) collective-permute-start(bf16[512,128]{1,0:T(8,128)(2,1)S(1)} %get-tuple-element.103), channel_id=1, source_target_pairs={{0,4},{1,5},{2,6},{3,7},{4,0},{5,1},{6,2},{7,3},{8,12},{9,13},{10,... | collective-permute-start | bytes 393224 | tf_op jit(solution)/shard_map/ppermute | solution.py:455
  514.2 11.6 %collective-permute-start.42 = (bf16[512,128]{1,0:T(8,128)(2,1)S(1)}, bf16[512,128]{1,0:T(8,128)(2,1)S(1)}, u32[]{:S(2)}, u32[]{:S(2)}) collective-permute-start(bf16[512,128]{1,0:T(8,128)(2,1)S(1)} %get-tuple-element.99), channel_id=1, source_target_pairs={{0,4},{1,5},{2,6},{3,7},{4,0},{5,1},{6,2},{7,3},{8,12},{9,13},{10,... | collective-permute-start | bytes 393224 | tf_op jit(solution)/shard_map/ppermute | solution.py:455
  517.9 8.0 %collective-permute-start.45 = (bf16[512,128]{1,0:T(8,128)(2,1)S(1)}, bf16[512,128]{1,0:T(8,128)(2,1)S(1)}, u32[]{:S(2)}, u32[]{:S(2)}) collective-permute-start(bf16[512,128]{1,0:T(8,128)(2,1)S(1)} %get-tuple-element.98), channel_id=1, source_target_pairs={{0,2},{1,3},{2,4},{3,5},{4,6},{5,7},{6,0},{7,1},{8,10},{9,11},{10,... | collective-permute-start | bytes 393224 | tf_op jit(solution)/shard_map/ppermute | solution.py:455
  531.4 6.5 collective-permute-start.47
  532.8 8.8 %collective-permute-start.49 = (f32[4,24,576]{2,1,0:T(8,128)S(1)}, f32[4,24,576]{2,1,0:T(8,128)S(1)}, u32[]{:S(2)}, u32[]{:S(2)}) collective-permute-start(f32[4,24,576]{2,1,0:T(8,128)S(1)} %get-tuple-element.84), channel_id=1, source_target_pairs={{0,24},{8,16},{16,8},{24,0},{1,25},{9,17},{17,9},{25,1},{2,26},{10... | collective-permute-start | bytes 663560 | tf_op jit(solution)/shard_map/ppermute | solution.py:610
  534.4 8.8 %collective-permute-start.48 = (f32[4,24,576]{2,1,0:T(8,128)S(1)}, f32[4,24,576]{2,1,0:T(8,128)S(1)}, u32[]{:S(2)}, u32[]{:S(2)}) collective-permute-start(f32[4,24,576]{2,1,0:T(8,128)S(1)} %get-tuple-element.85), channel_id=1, source_target_pairs={{0,16},{8,24},{16,0},{24,8},{1,17},{9,25},{17,1},{25,9},{2,18},{10... | collective-permute-start | bytes 663560 | tf_op jit(solution)/shard_map/ppermute | solution.py:610
  543.8 6.1 collective-permute-start.52
  545.4 5.8 collective-permute-start.51
  545.5 5.7 collective-permute-start.50
  552.5 125.7 %copy-start.1 = (f32[32,12]{0,1:T(8,128)S(1)}, f32[32,12]{0,1:T(8,128)}, u32[]{:S(2)}) copy-start(f32[32,12]{0,1:T(8,128)} %param.22) | copy-start | bytes 4612
  552.8 124.9 %copy-start.53 = (f32[24]{0:T(128)S(1)}, f32[24]{0:T(128)}, u32[]{:S(2)}) copy-start(f32[24]{0:T(128)} %param.32) | copy-start | bytes 292
  552.8 124.9 %copy-start.54 = (f32[24]{0:T(128)S(1)}, f32[24]{0:T(128)}, u32[]{:S(2)}) copy-start(f32[24]{0:T(128)} %param.30) | copy-start | bytes 292
  553.0 125.2 %copy-start.35 = (f32[3,3,8,768]{3,2,0,1:T(8,128)}, f32[3,3,8,768]{3,2,0,1:T(8,128)S(1)}, u32[]{:S(2)}) copy-start(f32[3,3,8,768]{3,2,0,1:T(8,128)S(1)} %copy.60) | copy-start | bytes 663556
  (55 other events, 1392.8 us)
Sparse Core Ops, SparseCore 0:
  11.5 67.1 all-gather.4
  81.6 55.4 all-gather.6
  140.2 74.6 all-gather.8
  217.8 57.9 all-gather.10
  296.3 94.9 reduce-scatter.3
  396.6 102.8 reduce-scatter.7
  505.1 120.9 reduce-scatter.5
